TPU v7x, 32 devices: a whole 2x2x4 slice. The times are simulated.
32 devices in a mesh: px: 16 (over z, x, core), pz: 2 (over y).
Axes of the slice: x: 2, y: 2, z: 4, core: 2. Of those that a mesh axis runs over, the one named last changes fastest.
Arguments:
- scalar_field: float32 [768, 384, 384], P('px', 'pz'), may hold values from -6 to 6
- prev_tendency: float32 [768, 384, 384], P('px', 'pz'), may hold values from -3 to 3
- velocity_u: bfloat16 [768, 384, 384], P('px', 'pz'), may hold values from -6 to 6
- velocity_v: bfloat16 [768, 384, 384], P('px', 'pz'), may hold values from -1.5 to 1.5
- velocity_w: bfloat16 [768, 384, 384], P('px', 'pz'), may hold values from -3 to 3
Outputs:
- scalar_next: float32 [768, 384, 384], P('px', 'pz')
- tendency: float32 [768, 384, 384], P('px', 'pz')
All inputs are finite; a program needn't handle non-finite values.
Results may differ from a plain program's by a relative error of at most 0.0003.
Values may be sent and summed in bfloat16 or wider, within the bound.
No kernel may reach another device: no remote copies, remote signals or barrier semaphores. Data moves between devices by JAX's collectives and lax.ppermute only.
A program may use at most 512 MiB of HBM per device.

v0:
```python
import jax
import jax.numpy as jnp
from jax import lax
from jax.sharding import PartitionSpec as P

KAPPA = 1.0 / (550.0 * 0.71)
DT_STEP = 0.005
GAMMA_RK = 8.0 / 15.0
ZETA_RK = -17.0 / 60.0
LENGTH_X = 4.0 * 3.141592653589793
LENGTH_Z = 4.0 * 3.141592653589793 / 3.0


def wall_operator(points):
    intervals = points - 1
    row_index = jnp.arange(points, dtype=jnp.int32)
    row_grid = row_index[:, None]
    col_grid = row_index[None, :]
    node_angle = row_index.astype(jnp.float32) * (jnp.pi / intervals)
    node_values = jnp.cos(node_angle)
    half_step = jnp.pi / (2.0 * intervals)
    sum_angle = (row_grid + col_grid).astype(jnp.float32) * half_step
    differ = (row_grid - col_grid).astype(jnp.float32) * half_step
    node_gap = -2.0 * jnp.sin(sum_angle) * jnp.sin(differ)
    same_node = row_grid == col_grid
    safe_gap = jnp.where(same_node, jnp.float32(1.0), node_gap)
    interior = (row_index > 0) & (row_index < intervals)
    weight = jnp.where(interior, jnp.float32(1.0), jnp.float32(2.0))
    parity = (1 - 2 * ((row_grid + col_grid) % 2)).astype(jnp.float32)
    damping = jnp.square(jnp.sin(node_angle))
    off_diagonal = damping[:, None] * (weight[:, None] / weight[None, :]) * parity / safe_gap
    diagonal = jnp.where(interior, -0.5 * node_values, jnp.float32(0.0))
    full = jnp.where(same_node, diagonal[:, None] * jnp.ones_like(off_diagonal), off_diagonal)
    return jnp.where(interior[:, None], full, jnp.float32(0.0))


def fourier_tables(extent, length):
    mode_count = extent // 3
    point_index = jnp.arange(extent, dtype=jnp.int32)
    mode_index = jnp.arange(mode_count, dtype=jnp.int32)
    phase_index = point_index[:, None] * mode_index[None, :] % extent
    phase = phase_index.astype(jnp.float32) * (2.0 * jnp.pi / extent)
    cosine = jnp.cos(phase)
    sine = jnp.sin(phase)
    wavenumber = mode_index.astype(jnp.float32) * (2.0 * jnp.pi / length)
    factor = 2.0 / extent
    forward = jnp.concatenate([cosine, sine], axis=1)
    first_rows = jnp.concatenate(
        [-factor * wavenumber * sine, factor * wavenumber * cosine], axis=1
    )
    square_wave = KAPPA * factor * wavenumber * wavenumber
    second_rows = jnp.concatenate([-square_wave * cosine, -square_wave * sine], axis=1)
    inverse = jnp.concatenate([first_rows, second_rows], axis=0)
    return (forward, inverse)


def along_first(field):
    extent = field.shape[0]
    forward, inverse = fourier_tables(extent, LENGTH_X)
    flattened = field.reshape(extent, -1)
    spectrum = lax.dot_general(
        forward, flattened, (((0,), (0,)), ((), ())), precision=lax.Precision.HIGHEST
    )
    results = jnp.dot(inverse, spectrum, precision=lax.Precision.HIGHEST)
    return (results[:extent].reshape(field.shape), results[extent:].reshape(field.shape))


def along_last(field):
    extent = field.shape[2]
    forward, inverse = fourier_tables(extent, LENGTH_Z)
    flattened = field.reshape(-1, extent)
    spectrum = jnp.dot(flattened, forward, precision=lax.Precision.HIGHEST)
    results = lax.dot_general(
        spectrum, inverse, (((1,), (1,)), ((), ())), precision=lax.Precision.HIGHEST
    )
    return (results[:, :extent].reshape(field.shape), results[:, extent:].reshape(field.shape))


def body(scalar_field, prev_tendency, velocity_u, velocity_v, velocity_w):
    z_first, z_diffusion = along_last(scalar_field)
    normal = lax.all_to_all(scalar_field, "pz", split_axis=2, concat_axis=1, tiled=True)
    wall_matrix = wall_operator(normal.shape[1])
    wall_slope = jnp.einsum("ij,ajb->aib", wall_matrix, normal, precision=lax.Precision.HIGHEST)
    stream_u = velocity_u.astype(jnp.float32)
    slope_home = lax.all_to_all(wall_slope, "pz", split_axis=1, concat_axis=2, tiled=True)
    x_pencil = lax.all_to_all(scalar_field, "px", split_axis=2, concat_axis=0, tiled=True)
    x_first, x_diffusion = along_first(x_pencil)
    home_first, home_diffusion = (
        lax.all_to_all(x_first, "px", split_axis=0, concat_axis=2, tiled=True),
        lax.all_to_all(x_diffusion, "px", split_axis=0, concat_axis=2, tiled=True),
    )
    streamwise = stream_u * home_first + home_diffusion
    forcing = (
        streamwise
        + velocity_v.astype(jnp.float32) * slope_home
        + velocity_w.astype(jnp.float32) * z_first
        + z_diffusion
    )
    tendency = DT_STEP * forcing
    scalar_next = scalar_field + GAMMA_RK * tendency + ZETA_RK * prev_tendency
    return (scalar_next, tendency)


def solution(mesh):
    return jax.shard_map(
        body,
        mesh=mesh,
        in_specs=(
            P("px", "pz", None),
            P("px", "pz", None),
            P("px", "pz", None),
            P("px", "pz", None),
            P("px", "pz", None),
        ),
        out_specs=(P("px", "pz", None), P("px", "pz", None)),
        check_vma=False,
    )
```

profile of v0, /device:TPU:15, one launch (start us, length us, event | category | flops | bytes accessed | tf_op | source)
XLA Modules:
  0.0 1850.5 jit_solution(8589513416588852409)
XLA Ops:
  0.6 19.2 %copy.72 = f32[48,192,384]{1,0,2:T(8,128)} copy(f32[48,192,384]{2,1,0:T(8,128)} %param.5) | data formatting | bytes 28311552 | tf_op args[0]
  19.8 223.1 %all_to_all.87 = f32[48,192,384]{1,0,2:T(8,128)} all-to-all(f32[48,192,384]{1,0,2:T(8,128)} %copy.72), channel_id=1, replica_groups=mesh['px'=16,'pz'=2] {'pz'}, dimensions={2} | all-to-all | bytes 28311552 | tf_op jit(solution)/shard_map/all_to_all | solution.py:81
  254.3 32.0 %copy.95 = f32[48,192,2,192]{1,2,3,0:T(2,128)} copy(f32[48,192,2,192]{1,0,3,2:T(8,128)} %bitcast.61) | data formatting | bytes 28311552 | tf_op jit(solution)/shard_map/all_to_all | solution.py:81
  286.3 21.9 %all_to_all.77 = f32[48,384,192]{1,2,0:T(8,128)} reshape(f32[48,2,192,192]{2,1,3,0:T(2,128)} %bitcast.62) | data formatting | bytes 28311552 | tf_op jit(solution)/shard_map/all_to_all | solution.py:81
  308.2 30.8 %fusion.39 = f32[384,9216]{0,1} fusion(f32[384,9216]{0,1:T(8,128)} %bitcast.63, f32[384,384]{1,0:T(8,128)S(1)} %fusion.108), kind=kOutput, calls=%fused_computation.53 | convolution fusion | flops 16307453952 | bytes 28901376
  339.0 18.9 %copy.84 = f32[48,384,192]{2,0,1:T(8,128)} copy(f32[48,384,192]{1,2,0:T(8,128)} %bitcast.64) | data formatting | bytes 28311552 | tf_op jit(solution)/shard_map/ij,ajb->aib/transpose | solution.py:83
  357.9 299.1 %all-to-all-done = f32[48,192,384]{1,0,2:T(8,128)} async-done(((f32[48,192,384]{1,0,2:T(8,128)}), f32[48,192,384]{1,0,2:T(8,128)}, u32[]{:S(2)}, u32[]{:S(2)}) %all-to-all-start) | async-done | bytes 14155808 | tf_op jit(solution)/shard_map/all_to_all | solution.py:86
  657.0 11.9 all-to-all-start.4
  679.8 31.0 %copy.74 = f32[16,48,192,24]{1,0,3,2:T(8,128)} copy(f32[16,48,192,24]{2,1,3,0:T(8,128)} %bitcast.2) | data formatting | bytes 28311552 | tf_op jit(solution)/shard_map/all_to_all | solution.py:86
  710.7 30.3 %reshape.82 = f32[768,4608]{0,1:T(8,128)} reshape(f32[16,48,192,24]{1,0,3,2:T(8,128)} %copy.74) | data formatting | bytes 28311552 | tf_op jit(solution)/shard_map/reshape | solution.py:60
  741.1 57.9 %fusion.11 = f32[512,4608]{1,0:T(8,128)S(1)} fusion(f32[768,4608]{0,1:T(8,128)} %reshape.82, f32[768,256]{1,0:T(8,128)S(1)} %get-tuple-element.26, f32[768,256]{1,0:T(8,128)S(1)} %get-tuple-element.25), kind=kOutput, calls=%fused_computation.17 | convolution fusion | flops 21743665152 | bytes 25165824 | tf_op jit(solution)/shard_map/dot_general | solution.py:61
  799.0 50.2 %fusion.3 = f32[1536,4608]{1,0:T(8,128)} fusion(f32[512,4608]{1,0:T(8,128)S(1)} %fusion.11, f32[768,256]{1,0:T(8,128)S(1)} %copy-done.1, f32[768,256]{1,0:T(8,128)S(1)} %copy-done, f32[768,256]{1,0:T(8,128)S(1)} %get-tuple-element.27, f32[768,256]{1,0:T(8,128)S(1)} %get-tuple-element.28), kind=kOutput, calls=%fused_computation.9 | convolution fusion | flops 43488903168 | bytes 40894464 | tf_op jit(solution)/shard_map/dot_general | solution.py:64
  849.1 18.6 %fusion.95 = (f32[768,4608]{1,0:T(8,128)}, f32[768,4608]{1,0:T(8,128)}) fusion(f32[1536,4608]{1,0:T(8,128)} %fusion.3), kind=kLoop, calls=%fused_computation.125 | loop fusion | bytes 56623104 | tf_op jit(solution)/shard_map/slice | solution.py:65
  867.7 15.1 copy.75
  882.8 18.9 %copy.76 = f32[768,192,24]{1,2,0:T(8,128)} copy(f32[768,192,24]{0,2,1:T(8,128)} %bitcast.67) | data formatting | bytes 28311552 | tf_op jit(solution)/shard_map/reshape | solution.py:65
  906.9 15.1 copy.78
  922.0 18.7 %copy.79 = f32[768,192,24]{1,2,0:T(8,128)} copy(f32[768,192,24]{0,2,1:T(8,128)} %bitcast.68) | data formatting | bytes 28311552 | tf_op jit(solution)/shard_map/reshape | solution.py:65
  940.7 373.3 %all-to-all-done.1 = f32[768,192,24]{1,2,0:T(8,128)} async-done(((f32[768,192,24]{1,2,0:T(8,128)}), f32[768,192,24]{1,2,0:T(8,128)}, u32[]{:S(2)}, u32[]{:S(2)}) %all-to-all-start.1) | async-done | bytes 14155808 | tf_op jit(solution)/shard_map/all_to_all | solution.py:89
  1319.1 16.8 copy.89
  1338.3 28.7 %fusion.58 = f32[256,9216]{1,0:T(8,128)} fusion(f32[9216,384]{1,0:T(8,128)} %bitcast.60, f32[384,128]{1,0:T(8,128)S(1)} %get-tuple-element.20, f32[384,128]{1,0:T(8,128)S(1)} %get-tuple-element.21), kind=kOutput, calls=%fused_computation.68 | convolution fusion | flops 10871734272 | bytes 23986176 | tf_op jit(solution)/shard_map/dot_general | solution.py:72
  1367.0 50.6 %fusion.21 = f32[9216,768]{1,0:T(8,128)S(1)} fusion(f32[256,9216]{1,0:T(8,128)} %fusion.58, f32[384,128]{1,0:T(8,128)S(1)} %get-tuple-element.19, f32[384,128]{1,0:T(8,128)S(1)} %get-tuple-element.18, f32[384,128]{1,0:T(8,128)S(1)} %get-tuple-element.22, f32[384,128]{1,0:T(8,128)S(1)} %broadcast_multiply_fusion.7), kind=kOutput, calls=%fused_computation.33 | convolution fusion | flops 21743861760 | bytes 38535168 | tf_op jit(solution)/shard_map/dot_general | solution.py:73
  1427.5 16.8 copy.87
  1444.3 16.7 copy.88
  1494.7 16.8 copy.90
  1511.5 20.4 %copy.85 = f32[48,2,192,192]{2,3,1,0:T(8,128)} copy(f32[48,2,192,192]{3,0,2,1:T(8,128)} %bitcast.17) | data formatting | bytes 28311552 | tf_op jit(solution)/shard_map/all_to_all | solution.py:85
  1531.9 12.7 copy.77
  1544.6 181.3 %all-to-all-done.2 = f32[768,192,24]{1,2,0:T(8,128)} async-done(((f32[768,192,24]{1,2,0:T(8,128)}), f32[768,192,24]{1,2,0:T(8,128)}, u32[]{:S(2)}, u32[]{:S(2)}) %all-to-all-start.2) | async-done | bytes 14155808 | tf_op jit(solution)/shard_map/all_to_all | solution.py:90
  1725.9 12.8 copy.80
  1738.7 51.8 %broadcast_multiply_fusion = (f32[48,192,384]{1,2,0:T(8,128)}, f32[48,192,384]{1,2,0:T(8,128)}) fusion(f32[48,192,384]{1,2,0:T(8,128)} %copy.88, f32[48,192,384]{1,2,0:T(8,128)} %copy.87, bf16[48,192,384]{1,2,0:T(8,128)(2,1)} %copy.86, f32[48,2,192,192]{2,3,1,0:T(8,128)} %copy.85, bf16[48,192,384]{1,2,0:T(8,128)(2,1)} %copy.81, f32[48,192,16,24]{1,3,2,0:T(8,128)} %copy.80, ...), kind=kLoop, calls=%fused_computation.8 | loop fusion | flops 38928384 | bytes 120324096 | tf_op jit(solution)/shard_map/mul | solution.py:99
  1790.6 25.5 %multiply_add_fusion = f32[48,192,384]{1,2,0:T(8,128)} fusion(f32[48,192,384]{1,2,0:T(8,128)} %copy.90, f32[48,192,384]{1,2,0:T(8,128)} %copy.89, f32[48,192,384]{1,2,0:T(8,128)} %get-tuple-element.11), kind=kLoop, calls=%fused_computation.7 | loop fusion | flops 14155776 | bytes 56623104 | tf_op jit(solution)/shard_map/add | solution.py:100
  1816.0 17.0 copy.91
  1833.0 17.0 copy.92
  (28 shorter events, 78.5 us)
Async XLA Ops:
  242.9 414.2 %all-to-all-start = ((f32[48,192,384]{1,0,2:T(8,128)}), f32[48,192,384]{1,0,2:T(8,128)}, u32[]{:S(2)}, u32[]{:S(2)}) async-start(f32[48,192,384]{1,0,2:T(8,128)} %copy.72), calls=%async_computation | async-start | bytes 37748736 | tf_op jit(solution)/shard_map/all_to_all | solution.py:86
  657.0 244.7 %all-to-all-start.4 = ((f32[48,384,192]{2,0,1:T(8,128)}), f32[48,384,192]{2,0,1:T(8,128)}, u32[]{:S(2)}, u32[]{:S(2)}) async-start(f32[48,384,192]{2,0,1:T(8,128)} %copy.84), calls=%async_computation.4 | async-start | bytes 37748736 | tf_op jit(solution)/shard_map/all_to_all | solution.py:85
  741.1 57.9 %copy-start = (f32[768,256]{1,0:T(8,128)S(1)}, f32[768,256]{1,0:T(8,128)}, u32[]{:S(2)}) copy-start(f32[768,256]{1,0:T(8,128)} %get-tuple-element.16) | copy-start | bytes 2359300
  741.1 57.9 %copy-start.1 = (f32[768,256]{1,0:T(8,128)S(1)}, f32[768,256]{1,0:T(8,128)}, u32[]{:S(2)}) copy-start(f32[768,256]{1,0:T(8,128)} %get-tuple-element.17) | copy-start | bytes 2359300
  901.7 412.2 %all-to-all-start.1 = ((f32[768,192,24]{1,2,0:T(8,128)}), f32[768,192,24]{1,2,0:T(8,128)}, u32[]{:S(2)}, u32[]{:S(2)}) async-start(f32[768,192,24]{1,2,0:T(8,128)} %copy.76), calls=%async_computation.1 | async-start | bytes 37748736 | tf_op jit(solution)/shard_map/all_to_all | solution.py:89
  1314.0 412.0 %all-to-all-start.2 = ((f32[768,192,24]{1,2,0:T(8,128)}), f32[768,192,24]{1,2,0:T(8,128)}, u32[]{:S(2)}, u32[]{:S(2)}) async-start(f32[768,192,24]{1,2,0:T(8,128)} %copy.79), calls=%async_computation.2 | async-start | bytes 37748736 | tf_op jit(solution)/shard_map/all_to_all | solution.py:90
where the time goes:
time: 1860 us; the launch traced here: 1850 us
  waiting for transfers between devices  854 us (46%)
  local copies, waits for them, and re-layouts  430 us (23%)
  blocking collectives  223 us (12%)
  matrix products  218 us (12%)
  other arithmetic  94.8 us (5%)
  starting transfers between devices  29.3 us (2%)
    all_to_all x1, waiting for transfers between devices, body(): lax.all_to_all(x_first, 'px', split_axis=0, concat_axis=2, tiled=True)  373 us
    all_to_all x1, waiting for transfers between devices, body(): lax.all_to_all(scalar_field, 'px', split_axis=2, concat_axis=0, tiled=True)  299 us
    all_to_all x1, blocking collectives, body(): lax.all_to_all(scalar_field, 'pz', split_axis=2, concat_axis=1, tiled=True)  223 us
    all_to_all x1, waiting for transfers between devices, body(): lax.all_to_all(x_diffusion, 'px', split_axis=0, concat_axis=2, tiled=True)  181 us
    unnamed x12, local copies, waits for them, and re-layouts  120 us
    dot_general x1, matrix products, along_first(): lax.dot_general(forward, flattened, (((0,), (0,)), ((), ())), precision=l...  57.9 us
    all_to_all x2, local copies, waits for them, and re-layouts, body(): lax.all_to_all(scalar_field, 'pz', split_axis=2, concat_axis=1, tiled=True)  53.9 us
    mul x1, other arithmetic, body(): tendency = DT_STEP * forcing  51.8 us
  transfers between devices with their start and end apart: 4, of which 3 were waited for; matrix products, arithmetic and copies ran while one was open for 31% of the time, Pallas kernels for 0%

commit v1 on v0

v1 whole, which is shorter than its diff:
```python
import functools

import jax
import jax.numpy as jnp
import ml_dtypes
import numpy as np
from jax import lax
from jax.experimental import pallas as pl
from jax.experimental.pallas import tpu as pltpu
from jax.sharding import PartitionSpec as P

KAPPA = 1.0 / (550.0 * 0.71)
DT_STEP = 0.005
GAMMA_RK = 8.0 / 15.0
ZETA_RK = -17.0 / 60.0
LENGTH_X = 4.0 * 3.141592653589793
LENGTH_Z = 4.0 * 3.141592653589793 / 3.0

F32 = jnp.float32
BF16 = jnp.bfloat16
VMEM = 56 << 20

SCALAR_BOUND = 6.0
VELOCITY_BOUND = 6.0
CODE_TOP = 120.0
SCALAR_RATE = CODE_TOP / (0.5 * SCALAR_BOUND)
STREAM_UNIT = 8.0
LOG2E = 1.4426950408889634


def wall_table(points):
    j = np.arange(points)
    angle = np.pi * j / (points - 1)
    node = np.cos(angle)
    weight = np.where((j == 0) | (j == points - 1), 2.0, 1.0)
    half = 0.5 * np.pi / (points - 1)
    gap = -2.0 * np.sin((j[:, None] + j[None, :]) * half) * np.sin((j[:, None] - j[None, :]) * half)
    gap[j, j] = 1.0
    parity = 1.0 - 2.0 * ((j[:, None] + j[None, :]) % 2)
    table = (np.sin(angle) ** 2)[:, None] * (weight[:, None] / weight[None, :]) * parity / gap
    table[j, j] = -0.5 * node
    table[0, :] = 0.0
    table[-1, :] = 0.0
    return table


def fourier_kernels(extent, length):
    mode = np.arange(extent // 3)
    wave = mode * (2.0 * np.pi / length)
    phase = 2.0 * np.pi * (np.outer(np.arange(extent), mode) % extent) / extent
    first = -(2.0 / extent) * (np.sin(phase) @ wave)
    second = -(2.0 * KAPPA / extent) * (np.cos(phase) @ (wave * wave))
    return first, second


def circulant(column):
    n = column.shape[0]
    i = np.arange(n)
    return column[(i[:, None] - i[None, :]) % n]


def two_terms(table):
    table = np.asarray(table, np.float32)
    high = table.astype(ml_dtypes.bfloat16)
    low = (table - high.astype(np.float32)).astype(ml_dtypes.bfloat16)
    return np.stack([high, low])


def encode_scalar(x):
    size = jnp.exp2(SCALAR_RATE * jnp.abs(x) - CODE_TOP)
    return jnp.where(x < 0, -size, size)


def decode_scalar(b):
    size = (jnp.log(jnp.abs(b)) * LOG2E + CODE_TOP) * (1.0 / SCALAR_RATE)
    return jnp.where(b < 0, -size, size)


def encode_stream(x, rate):
    size = jnp.exp2((rate * LOG2E) * jnp.log(1.0 + jnp.abs(x) * (1.0 / STREAM_UNIT)) - CODE_TOP)
    return jnp.where(x < 0, -size, size)


def decode_stream(b, rate):
    size = STREAM_UNIT * (jnp.exp2((jnp.log(jnp.abs(b)) * LOG2E + CODE_TOP) * (1.0 / rate)) - 1.0)
    return jnp.where(b < 0, -size, size)


def split(x):
    high = x.astype(BF16)
    return high, (x - high.astype(F32)).astype(BF16)


def dot(a, b):
    return jnp.dot(a, b, preferred_element_type=F32)


def dot3(a_high, a_low, b_high, b_low):
    return dot(a_high, b_high) + dot(a_high, b_low) + dot(a_low, b_high)


def params(**kw):
    return pltpu.CompilerParams(vmem_limit_bytes=VMEM, **kw)


def cost(flops, moved):
    return pl.CostEstimate(flops=int(flops), bytes_accessed=int(moved), transcendentals=0)


STEP = 16


def pack_kernel(f_ref, u_ref, g_ref, w_ref):
    code = encode_scalar(f_ref[...])
    g_ref[...] = jnp.swapaxes(code, 0, 1).astype(BF16).reshape(g_ref.shape)
    u = jnp.swapaxes(u_ref[...].astype(F32), 0, 1)
    w_ref[...] = u.astype(BF16).reshape(w_ref.shape)


def pack(f, u, first_row, rows, shares):
    nx, ny, nz = f.shape
    each = rows // shares
    per = STEP // each
    out = jax.ShapeDtypeStruct((shares, each, nx, nz), BF16)
    base = first_row // STEP
    return pl.pallas_call(
        pack_kernel,
        grid=(rows // STEP,),
        in_specs=[pl.BlockSpec((nx, STEP, nz), lambda i: (0, base + i, 0))] * 2,
        out_specs=[pl.BlockSpec((per, each, nx, nz), lambda i: (i, 0, 0, 0))] * 2,
        out_shape=[out, out],
        compiler_params=params(),
        cost_estimate=cost(0, rows * nx * nz * 10),
    )(f, u)


def code_kernel(f_ref, h_ref):
    h_ref[...] = encode_scalar(f_ref[...]).astype(BF16)


def code(f, first, planes):
    _, ny, nz = f.shape
    step = 4
    base = first // step
    return pl.pallas_call(
        code_kernel,
        grid=(planes // step,),
        in_specs=[pl.BlockSpec((step, ny, nz), lambda i: (base + i, 0, 0))],
        out_specs=pl.BlockSpec((step, ny, nz), lambda i: (i, 0, 0)),
        out_shape=jax.ShapeDtypeStruct((planes, ny, nz), BF16),
        compiler_params=params(),
        cost_estimate=cost(0, planes * ny * nz * 6),
    )(f)


def stream_kernel(n_in, n_out, rate, table_ref, *refs):
    f_refs, u_refs, s_refs = refs[:n_in], refs[n_in:n_in + n_out], refs[n_in + n_out:]
    rows = refs[0].shape[1]
    nz = refs[0].shape[3]
    columns = []
    for k in range(rows):
        blocks = [r[:, k].astype(F32).reshape(-1, nz) for r in f_refs]
        columns.append(jnp.concatenate(blocks, axis=0) if n_in > 1 else blocks[0])
    field = decode_scalar(jnp.concatenate(columns, axis=1))
    high, low = split(field)
    start = 0
    for o in range(n_out):
        parts, nx = u_refs[o].shape[0], u_refs[o].shape[2]
        bunch = 4
        for s in range(0, parts, bunch):
            tall = bunch * nx
            pair = []
            for which in range(2):
                t_high = table_ref[0, which, pl.ds(start, tall), :]
                t_low = table_ref[1, which, pl.ds(start, tall), :]
                pair.append(dot3(t_high, t_low, high, low))
            for k in range(rows):
                cols = slice(k * nz, (k + 1) * nz)
                u = u_refs[o][s:s + bunch, k].astype(F32).reshape(tall, nz)
                value = u * pair[0][:, cols] + pair[1][:, cols]
                coded = encode_stream(value, rate).astype(BF16)
                s_refs[o][s:s + bunch, k] = coded.reshape(bunch, nx, nz)
            start += tall


def stream(table, fields, speeds, rate):
    parts, rows, nx, nz = fields[0].shape
    n_in, n_out = len(fields), len(speeds)
    step = 2 if rows % 2 == 0 else 1
    block = pl.BlockSpec((parts, step, nx, nz), lambda i: (0, i, 0, 0))
    whole = pl.BlockSpec(table.shape, lambda i: (0, 0, 0, 0), pipeline_mode=pl.Buffered(1))
    points = table.shape[2] * table.shape[3]
    moved = 2 * (n_in + 2 * n_out) * parts * rows * nx * nz
    return pl.pallas_call(
        functools.partial(stream_kernel, n_in, n_out, rate),
        grid=(rows // step,),
        in_specs=[whole] + [block] * (n_in + n_out),
        out_specs=[block] * n_out,
        out_shape=[jax.ShapeDtypeStruct(fields[0].shape, BF16)] * n_out,
        compiler_params=params(),
        cost_estimate=cost(12 * points * rows * nz, moved),
    )(table, *fields, *speeds)


def local_kernel(wall_ref, span_ref, f_ref, h_ref, v_ref, w_ref, p_ref, *refs):
    next_ref, tend_ref = refs[-2:]
    planes, ny, nz = f_ref.shape
    own = f_ref[...]
    other = decode_scalar(h_ref[...].astype(F32))
    own_high, own_low = split(own)
    other_high, other_low = split(other)

    def stack(a, b):
        return jnp.concatenate(
            [jnp.concatenate([a[x], b[x]], axis=0) for x in range(planes)], axis=1
        )

    y_high, y_low = stack(own_high, other_high), stack(own_low, other_low)
    slope = dot3(wall_ref[0], wall_ref[1], y_high, y_low)
    z_high, z_low = own_high.reshape(-1, nz), own_low.reshape(-1, nz)
    span = dot3(z_high, z_low, span_ref[0], span_ref[1])
    for x in range(planes):
        rows = slice(x * ny, (x + 1) * ny)
        forcing = (
            v_ref[x].astype(F32) * slope[:, x * nz:(x + 1) * nz]
            + w_ref[x].astype(F32) * span[rows, :nz]
            + span[rows, nz:]
        )
        tendency = DT_STEP * forcing
        tend_ref[x] = tendency
        next_ref[x] = own[x] + GAMMA_RK * tendency + ZETA_RK * p_ref[x]


def local(wall, span, f, h, v, w, prev, first, held):
    nx, ny, nz = f.shape
    planes = h.shape[0]
    step = 2
    base = first // step
    block = pl.BlockSpec((step, ny, nz), lambda i: (base + i, 0, 0))
    table = lambda t: pl.BlockSpec(t.shape, lambda i: (0, 0, 0), pipeline_mode=pl.Buffered(1))
    out = jax.ShapeDtypeStruct(f.shape, F32)
    keep = pl.BlockSpec(memory_space=pl.ANY)
    return pl.pallas_call(
        local_kernel,
        grid=(planes // step,),
        in_specs=[table(wall), table(span), block,
                  pl.BlockSpec((step, ny, nz), lambda i: (i, 0, 0)), block, block, block]
        + [keep] * len(held),
        out_specs=[block, block],
        out_shape=[out, out],
        input_output_aliases={7 + k: k for k in range(len(held))},
        compiler_params=params(),
        cost_estimate=cost(6 * planes * ny * nz * (2 * ny + 2 * nz), planes * ny * nz * 22),
    )(wall, span, f, h, v, w, prev, *held)


def merge_kernel(rate, s_ref, next_ref, tend_ref, next_out, tend_out):
    nx, step, nz = next_ref.shape
    coded = jnp.swapaxes(s_ref[...].astype(F32).reshape(step, nx, nz), 0, 1)
    add = DT_STEP * decode_stream(coded, rate)
    tend_out[...] = tend_ref[...] + add
    next_out[...] = next_ref[...] + GAMMA_RK * add


def merge(s, held, first_row, rate):
    nx, ny, nz = held[0].shape
    shares, each = s.shape[:2]
    per = STEP // each
    base = first_row // STEP
    block = pl.BlockSpec((nx, STEP, nz), lambda i: (0, base + i, 0))
    out = jax.ShapeDtypeStruct(held[0].shape, F32)
    return pl.pallas_call(
        functools.partial(merge_kernel, rate),
        grid=(shares * each // STEP,),
        in_specs=[pl.BlockSpec((per, each, nx, nz), lambda i: (i, 0, 0, 0)), block, block],
        out_specs=[block, block],
        out_shape=[out, out],
        input_output_aliases={1: 0, 2: 1},
        compiler_params=params(),
        cost_estimate=cost(0, shares * each * nx * nz * 18),
    )(s, *held)


CHUNKS = (32,) * 6
PIECES = 4
PLAIN = False


def body(px, pz, f, prev, u, v, w):
    nx, ny, nz = f.shape
    nxg = nx * px
    first, second = fourier_kernels(nxg, LENGTH_X)
    rate_bound = VELOCITY_BOUND * SCALAR_BOUND * np.abs(first).sum() + SCALAR_BOUND * np.abs(second).sum()
    rate = float(2 * CODE_TOP / np.log2(1.0 + 1.02 * rate_bound / STREAM_UNIT))
    k_first, k_second = circulant(first), circulant(second)
    z_first, z_second = (circulant(c) for c in fourier_kernels(nz, LENGTH_Z))
    span = jnp.asarray(two_terms(np.concatenate([z_first.T, z_second.T], axis=1)))
    walls = wall_table(ny * pz)
    mine = lax.axis_index("pz")
    wall_all = []
    for y in range(pz):
        rows = walls[y * ny:(y + 1) * ny]
        own = rows[:, y * ny:(y + 1) * ny]
        other = rows[:, (1 - y) * ny:(2 - y) * ny]
        wall_all.append(two_terms(np.concatenate([own, other], axis=1)))
    wall = lax.dynamic_index_in_dim(jnp.asarray(np.stack(wall_all)), mine, 0, keepdims=False)

    planes = nx // PIECES
    theirs = []
    for p in range(PIECES):
        theirs.append(lax.ppermute(code(f, p * planes, planes), "pz", [(0, 1), (1, 0)]))

    starts = np.concatenate([[0], np.cumsum(CHUNKS)])[:-1]
    streams = []
    if PLAIN:
        table = jnp.asarray(np.stack([two_terms(k_first), two_terms(k_second)], axis=1))
        for at, rows in zip(starts, CHUNKS):
            g, ut = pack(f, u, int(at), rows, px)
            g = lax.all_to_all(g, "px", 0, 0, tiled=True)
            ut = lax.all_to_all(ut, "px", 0, 0, tiled=True)
            (s,) = stream(table, [g], [ut], rate)
            streams.append(lax.all_to_all(s, "px", 0, 0, tiled=True))
    else:
        ring = px // 4
        quarter = nx * ring
        variants = []
        for order in ((1, 0, 2, 3), (2, 3, 1, 0)):
            pick = lambda m: np.concatenate(
                [np.concatenate([m[o * quarter:(o + 1) * quarter, q * quarter:(q + 1) * quarter] for q in order], axis=1)
                 for o in order[:2]], axis=0)
            variants.append(np.stack([two_terms(pick(k_first)), two_terms(pick(k_second))], axis=1))
        level = lax.axis_index("px") // ring
        table = lax.dynamic_index_in_dim(jnp.asarray(np.stack(variants)), level // 2, 0, keepdims=False)
        outer = (level == 0) | (level == 3)
        groups = [[l * ring + r for r in range(ring)] for l in range(4)]
        hop = lambda pairs: [(a * ring + r, b * ring + r) for a, b in pairs for r in range(ring)]
        inward, across, outward = hop([(0, 1), (3, 2)]), hop([(1, 2), (2, 1)]), hop([(1, 0), (2, 3)])
        for at, rows in zip(starts, CHUNKS):
            g, ut = pack(f, u, int(at), rows, ring)
            g = lax.all_to_all(g, "px", 0, 0, axis_index_groups=groups, tiled=True)
            ut = lax.all_to_all(ut, "px", 0, 0, axis_index_groups=groups, tiled=True)
            near = lax.ppermute(g, "px", inward)
            far = lax.ppermute(g, "px", across)
            near_u = lax.ppermute(ut, "px", inward)
            far_near = lax.ppermute(near, "px", across)
            s_own, s_near = stream(table, [g, near, far, far_near], [ut, near_u], rate)
            got = lax.ppermute(s_near, "px", outward)
            s = jnp.where(outer, got, s_own)
            streams.append(lax.all_to_all(s, "px", 0, 0, axis_index_groups=groups, tiled=True))

    held = ()
    for p in range(PIECES):
        held = tuple(local(wall, span, f, theirs[p], v, w, prev, p * planes, held))
    for at, s in zip(starts, streams):
        held = tuple(merge(s, held, int(at), rate))
    return held


def plain_wall(points):
    return jnp.asarray(wall_table(points), F32)


def plain_body(scalar_field, prev_tendency, velocity_u, velocity_v, velocity_w):
    highest = lax.Precision.HIGHEST
    z_tables = [circulant(c) for c in fourier_kernels(scalar_field.shape[2], LENGTH_Z)]
    z_first, z_diffusion = (
        jnp.einsum("ij,abj->abi", jnp.asarray(t, F32), scalar_field, precision=highest) for t in z_tables
    )
    normal = lax.all_to_all(scalar_field, "pz", split_axis=2, concat_axis=1, tiled=True)
    slope = jnp.einsum("ij,ajb->aib", plain_wall(normal.shape[1]), normal, precision=highest)
    slope = lax.all_to_all(slope, "pz", split_axis=1, concat_axis=2, tiled=True)
    pencil = lax.all_to_all(scalar_field, "px", split_axis=2, concat_axis=0, tiled=True)
    x_tables = [circulant(c) for c in fourier_kernels(pencil.shape[0], LENGTH_X)]
    x_first, x_diffusion = (
        lax.all_to_all(
            jnp.einsum("ij,jab->iab", jnp.asarray(t, F32), pencil, precision=highest),
            "px", split_axis=0, concat_axis=2, tiled=True,
        )
        for t in x_tables
    )
    forcing = (
        velocity_u.astype(F32) * x_first
        + x_diffusion
        + velocity_v.astype(F32) * slope
        + velocity_w.astype(F32) * z_first
        + z_diffusion
    )
    tendency = DT_STEP * forcing
    return scalar_field + GAMMA_RK * tendency + ZETA_RK * prev_tendency, tendency


def fits(px, pz, shape):
    nx, ny, nz = shape
    return px == 16 and pz == 2 and nx % 16 == 0 and ny == sum(CHUNKS) and nz % 128 == 0


def whole_body(px, pz, *arrays):
    if fits(px, pz, arrays[0].shape):
        return body(px, pz, *arrays)
    return plain_body(*arrays)


def solution(mesh):
    px, pz = mesh.shape["px"], mesh.shape["pz"]
    spec = P("px", "pz", None)
    return jax.shard_map(
        functools.partial(whole_body, px, pz),
        mesh=mesh,
        in_specs=(spec,) * 5,
        out_specs=(spec, spec),
        check_vma=False,
    )
```

time: 1860 us -> 632 us (0.34)
  the two profiles are of different devices: /device:TPU:15 before, /device:TPU:0 now
where the time goes in v1:
time: 632 us; the launch traced here: 622 us
  Pallas kernels  240 us (38%)
  waiting for transfers between devices  150 us (24%)
  starting transfers between devices  149 us (24%)
  blocking collectives  60.5 us (10%)
  other arithmetic  13.4 us (2%)
  local copies, waits for them, and re-layouts  8.09 us (1%)
    pallas_call x6, Pallas kernels, stream(): pl.pallas_call(functools.partial(stream_kernel, n_in, n_out, rate), grid=...  111 us
    all_to_all x3, blocking collectives, body(): g = lax.all_to_all(g, 'px', 0, 0, axis_index_groups=groups, tiled=True)  60.5 us
    pallas_call x4, Pallas kernels, local(): pl.pallas_call(local_kernel, grid=(planes // step,), in_specs=[table(wall...  56.3 us
    ppermute x6, waiting for transfers between devices, body(): near = lax.ppermute(g, 'px', inward)  54.8 us
    all_to_all x6, waiting for transfers between devices, body(): ut = lax.all_to_all(ut, 'px', 0, 0, axis_index_groups=groups, tiled=True)  36 us
    ppermute x6, starting transfers between devices, body(): near_u = lax.ppermute(ut, 'px', inward)  33.8 us
    pallas_call x6, Pallas kernels, merge(): pl.pallas_call(functools.partial(merge_kernel, rate), grid=(shares * each...  31.5 us
    ppermute x6, starting transfers between devices, body(): near = lax.ppermute(g, 'px', inward)  26.2 us
  transfers between devices with their start and end apart: 49, of which 14 were waited for; matrix products, arithmetic and copies ran while one was open for 3% of the time, Pallas kernels for 37%

profile of v1, /device:TPU:0, one launch (start us, length us, event | category | flops | bytes accessed | tf_op | source)
XLA Modules:
  0.0 621.6 jit_solution(8848668091795502527)
XLA Ops:
  4.6 20.1 %all_to_all.90.refs_0_ = bf16[4,8,48,384]{3,2,1,0:T(8,128)(2,1)S(1)} all-to-all(bf16[4,8,48,384]{3,2,1,0:T(8,128)(2,1)} %get-tuple-element.64), channel_id=1, replica_groups={{0,2,4,6},{8,10,12,14},{16,18,20,22},{24,26,28,30},{1,3,5,7},{9,11,13,1..., dimensions={0} | all-to-all | bytes 2359296 | tf_op jit(solution)/shard_map/all_to_all | solution.py:340
  32.8 12.0 %all-to-all-done.16.refs_4_ = bf16[4,8,48,384]{3,2,1,0:T(8,128)(2,1)} async-done(((bf16[4,8,48,384]{3,2,1,0:T(8,128)(2,1)}), bf16[4,8,48,384]{3,2,1,0:T(8,128)(2,1)}, u32[]{:S(2)}, u32[]{:S(2)}) %all-to-all-start.16) | async-done | bytes 1179680 | tf_op jit(solution)/shard_map/all_to_all | solution.py:341
  44.8 20.2 %all_to_all.91.refs_0_ = bf16[4,8,48,384]{3,2,1,0:T(8,128)(2,1)} all-to-all(bf16[4,8,48,384]{3,2,1,0:T(8,128)(2,1)} %get-tuple-element.60), channel_id=1, replica_groups={{0,2,4,6},{8,10,12,14},{16,18,20,22},{24,26,28,30},{1,3,5,7},{9,11,13,1..., dimensions={0} | all-to-all | bytes 2359296 | tf_op jit(solution)/shard_map/all_to_all | solution.py:340
  73.3 12.0 %all-to-all-done.13.refs_4_ = bf16[4,8,48,384]{3,2,1,0:T(8,128)(2,1)} async-done(((bf16[4,8,48,384]{3,2,1,0:T(8,128)(2,1)}), bf16[4,8,48,384]{3,2,1,0:T(8,128)(2,1)}, u32[]{:S(2)}, u32[]{:S(2)}) %all-to-all-start.13) | async-done | bytes 1179680 | tf_op jit(solution)/shard_map/all_to_all | solution.py:341
  85.3 20.2 %all_to_all.92.refs_0_ = bf16[4,8,48,384]{3,2,1,0:T(8,128)(2,1)} all-to-all(bf16[4,8,48,384]{3,2,1,0:T(8,128)(2,1)} %get-tuple-element.56), channel_id=1, replica_groups={{0,2,4,6},{8,10,12,14},{16,18,20,22},{24,26,28,30},{1,3,5,7},{9,11,13,1..., dimensions={0} | all-to-all | bytes 2359296 | tf_op jit(solution)/shard_map/all_to_all | solution.py:340
  112.9 11.9 %all-to-all-done.10.refs_4_ = bf16[4,8,48,384]{3,2,1,0:T(8,128)(2,1)S(1)} async-done(((bf16[4,8,48,384]{3,2,1,0:T(8,128)(2,1)}), bf16[4,8,48,384]{3,2,1,0:T(8,128)(2,1)S(1)}, u32[]{:S(2)}, u32[]{:S(2)}) %all-to-all-start.10) | async-done | bytes 1179680 | tf_op jit(solution)/shard_map/all_to_all | solution.py:341
  129.4 5.3 collective-permute-start.25
  139.5 5.8 all-to-all-done.6.refs_0_
  159.9 5.5 collective-permute-start.23
  167.8 17.5 %collective-permute-done.28.refs_5_ = bf16[4,8,48,384]{3,2,1,0:T(8,128)(2,1)} collective-permute-done((bf16[4,8,48,384]{3,2,1,0:T(8,128)(2,1)}, bf16[4,8,48,384]{3,2,1,0:T(8,128)(2,1)}, u32[]{:S(2)}, u32[]{:S(2)}) %collective-permute-start.28) | collective-permute-done | bytes 1179680 | tf_op jit(solution)/shard_map/ppermute | solution.py:344
  228.8 7.1 %collective-permute-done.23.refs_5_ = bf16[4,8,48,384]{3,2,1,0:T(8,128)(2,1)} collective-permute-done((bf16[4,8,48,384]{3,2,1,0:T(8,128)(2,1)}, bf16[4,8,48,384]{3,2,1,0:T(8,128)(2,1)}, u32[]{:S(2)}, u32[]{:S(2)}) %collective-permute-start.23) | collective-permute-done | bytes 1179680 | tf_op jit(solution)/shard_map/ppermute | solution.py:344
  235.9 5.4 collective-permute-start.18
  241.3 19.9 %collective-permute-done.15.refs_1_ = bf16[4,8,48,384]{3,2,1,0:T(8,128)(2,1)} collective-permute-done((bf16[4,8,48,384]{3,2,1,0:T(8,128)(2,1)}, bf16[4,8,48,384]{3,2,1,0:T(8,128)(2,1)}, u32[]{:S(2)}, u32[]{:S(2)}) %collective-permute-start.15) | collective-permute-done | bytes 1179680 | tf_op jit(solution)/shard_map/ppermute | solution.py:342
  261.1 5.4 collective-permute-start.10
  268.4 18.5 %shard_map.106 = (bf16[4,8,48,384]{3,2,1,0:T(8,128)(2,1)}, bf16[4,8,48,384]{3,2,1,0:T(8,128)(2,1)}) custom-call(bf16[2,2,384,768]{3,2,1,0:T(8,128)(2,1)} %dynamic-slice_bitcast_fusion.table_ref, bf16[4,8,48,384]{3,2,1,0:T(8,128)(2,1)} %copy-done.10, bf16[4,8,48,384]{3,2,1,0:T(8,128)(2,1)} %collective-permute-done.25.refs_1_, ...), custom_call_target="tpu_custom_call" | custom-call | flops 10871635968 | bytes 9437184 | tf_op jit(solution)/shard_map/pallas_call | solution.py:194
  292.6 18.5 %shard_map.104 = (bf16[4,8,48,384]{3,2,1,0:T(8,128)(2,1)}, bf16[4,8,48,384]{3,2,1,0:T(8,128)(2,1)}) custom-call(bf16[2,2,384,768]{3,2,1,0:T(8,128)(2,1)} %dynamic-slice_bitcast_fusion.table_ref, bf16[4,8,48,384]{3,2,1,0:T(8,128)(2,1)} %all_to_all.91.refs_0_, bf16[4,8,48,384]{3,2,1,0:T(8,128)(2,1)} %collective-permute-done.20.refs_1_, ...), custom_call_target="tpu_custom_call" | custom-call | flops 10871635968 | bytes 9437184 | tf_op jit(solution)/shard_map/pallas_call | solution.py:194
  316.2 8.4 %collective-permute-start.13 = (bf16[4,8,48,384]{3,2,1,0:T(8,128)(2,1)S(1)}, bf16[4,8,48,384]{3,2,1,0:T(8,128)(2,1)S(1)}, u32[]{:S(2)}, u32[]{:S(2)}) collective-permute-start(bf16[4,8,48,384]{3,2,1,0:T(8,128)(2,1)S(1)} %all-to-all-done.7.refs_4_), channel_id=1, source_target_pairs={{0,8},{2,10},{4,12},{6,14},{24,16},{26,18},{28,20},{30,22},{1,9},{... | collective-permute-start | bytes 3538952 | tf_op jit(solution)/shard_map/ppermute | solution.py:344
  327.7 18.4 %shard_map.102 = (bf16[4,8,48,384]{3,2,1,0:T(8,128)(2,1)}, bf16[4,8,48,384]{3,2,1,0:T(8,128)(2,1)}) custom-call(bf16[2,2,384,768]{3,2,1,0:T(8,128)(2,1)} %dynamic-slice_bitcast_fusion.table_ref, bf16[4,8,48,384]{3,2,1,0:T(8,128)(2,1)} %all_to_all.92.refs_0_, bf16[4,8,48,384]{3,2,1,0:T(8,128)(2,1)} %collective-permute-done.15.refs_1_, ...), custom_call_target="tpu_custom_call" | custom-call | flops 10871635968 | bytes 9437184 | tf_op jit(solution)/shard_map/pallas_call | solution.py:194
  351.6 6.0 collective-permute-start.8
  357.6 18.5 %collective-permute-done.5.refs_1_ = bf16[4,8,48,384]{3,2,1,0:T(8,128)(2,1)} collective-permute-done((bf16[4,8,48,384]{3,2,1,0:T(8,128)(2,1)S(1)}, bf16[4,8,48,384]{3,2,1,0:T(8,128)(2,1)}, u32[]{:S(2)}, u32[]{:S(2)}) %collective-permute-start.5) | collective-permute-done | bytes 1179680 | tf_op jit(solution)/shard_map/ppermute | solution.py:342
  376.1 5.5 collective-permute-start
  388.3 18.5 %shard_map.100 = (bf16[4,8,48,384]{3,2,1,0:T(8,128)(2,1)}, bf16[4,8,48,384]{3,2,1,0:T(8,128)(2,1)}) custom-call(bf16[2,2,384,768]{3,2,1,0:T(8,128)(2,1)} %dynamic-slice_bitcast_fusion.table_ref, bf16[4,8,48,384]{3,2,1,0:T(8,128)(2,1)} %copy-done.6, bf16[4,8,48,384]{3,2,1,0:T(8,128)(2,1)} %collective-permute-done.10.refs_1_, ...), custom_call_target="tpu_custom_call" | custom-call | flops 10871635968 | bytes 9437184 | tf_op jit(solution)/shard_map/pallas_call | solution.py:194
  413.8 12.2 %collective-permute-done.refs_1_ = bf16[4,8,48,384]{3,2,1,0:T(8,128)(2,1)} collective-permute-done((bf16[4,8,48,384]{3,2,1,0:T(8,128)(2,1)}, bf16[4,8,48,384]{3,2,1,0:T(8,128)(2,1)}, u32[]{:S(2)}, u32[]{:S(2)}) %collective-permute-start) | collective-permute-done | bytes 1179680 | tf_op jit(solution)/shard_map/ppermute | solution.py:342
  426.0 5.4 collective-permute-start.3
  436.7 18.5 %shard_map.98 = (bf16[4,8,48,384]{3,2,1,0:T(8,128)(2,1)}, bf16[4,8,48,384]{3,2,1,0:T(8,128)(2,1)}) custom-call(bf16[2,2,384,768]{3,2,1,0:T(8,128)(2,1)} %dynamic-slice_bitcast_fusion.table_ref, bf16[4,8,48,384]{3,2,1,0:T(8,128)(2,1)} %copy-done.7, bf16[4,8,48,384]{3,2,1,0:T(8,128)(2,1)} %collective-permute-done.5.refs_1_, ...), custom_call_target="tpu_custom_call" | custom-call | flops 10871635968 | bytes 9437184 | tf_op jit(solution)/shard_map/pallas_call | solution.py:194
  464.6 18.5 %shard_map.96 = (bf16[4,8,48,384]{3,2,1,0:T(8,128)(2,1)}, bf16[4,8,48,384]{3,2,1,0:T(8,128)(2,1)}) custom-call(bf16[2,2,384,768]{3,2,1,0:T(8,128)(2,1)} %dynamic-slice_bitcast_fusion.table_ref, bf16[4,8,48,384]{3,2,1,0:T(8,128)(2,1)} %all-to-all-done.refs_0_, bf16[4,8,48,384]{3,2,1,0:T(8,128)(2,1)} %collective-permute-done.refs_1_, ...), custom_call_target="tpu_custom_call" | custom-call | flops 10871635968 | bytes 9437184 | tf_op jit(solution)/shard_map/pallas_call | solution.py:194
  495.2 14.1 %shard_map.111 = (f32[48,192,384]{2,1,0:T(8,128)}, f32[48,192,384]{2,1,0:T(8,128)}) custom-call(bf16[2,192,384]{2,1,0:T(8,128)(2,1)} %dynamic-slice_bitcast_fusion.1.wall_ref, bf16[2,384,768]{2,1,0:T(8,128)(2,1)} %constant.49.clone.span_ref, f32[48,192,384]{2,1,0:T(8,128)} %f_ref.27, bf16[12,192,384]{2,1,0:T(8,128)(2,1)} %collective-permute-done.33.h_ref, ...), custom_call_target="tpu_custom_call" | custom-call | flops 6115295232 | bytes 19464192 | tf_op jit(solution)/shard_map/pallas_call | solution.py:243
  517.5 14.1 %shard_map.112 = (f32[48,192,384]{2,1,0:T(8,128)}, f32[48,192,384]{2,1,0:T(8,128)}) custom-call(bf16[2,192,384]{2,1,0:T(8,128)(2,1)} %dynamic-slice_bitcast_fusion.1.wall_ref, bf16[2,384,768]{2,1,0:T(8,128)(2,1)} %constant.49.clone.span_ref, f32[48,192,384]{2,1,0:T(8,128)} %f_ref.27, ...), custom_call_target="tpu_custom_call", output_to_operand_aliasing={{0}: (7, {}), {1}: (8, {})} | custom-call | flops 6115295232 | bytes 19464192 | tf_op jit(solution)/shard_map/pallas_call | solution.py:243
  542.3 14.0 %shard_map.113 = (f32[48,192,384]{2,1,0:T(8,128)}, f32[48,192,384]{2,1,0:T(8,128)}) custom-call(bf16[2,192,384]{2,1,0:T(8,128)(2,1)} %dynamic-slice_bitcast_fusion.1.wall_ref, bf16[2,384,768]{2,1,0:T(8,128)(2,1)} %constant.49.clone.span_ref, f32[48,192,384]{2,1,0:T(8,128)} %f_ref.27, ...), custom_call_target="tpu_custom_call", output_to_operand_aliasing={{0}: (7, {}), {1}: (8, {})} | custom-call | flops 6115295232 | bytes 19464192 | tf_op jit(solution)/shard_map/pallas_call | solution.py:243
  556.4 18.5 %collective-permute-done.30.h_ref = bf16[12,192,384]{2,1,0:T(8,128)(2,1)} collective-permute-done((bf16[12,192,384]{2,1,0:T(8,128)(2,1)}, bf16[12,192,384]{2,1,0:T(8,128)(2,1)}, u32[]{:S(2)}, u32[]{:S(2)}) %collective-permute-start.30) | collective-permute-done | bytes 1769504 | tf_op jit(solution)/shard_map/ppermute | solution.py:311
  574.8 14.0 %shard_map.114 = (f32[48,192,384]{2,1,0:T(8,128)}, f32[48,192,384]{2,1,0:T(8,128)}) custom-call(bf16[2,192,384]{2,1,0:T(8,128)(2,1)} %dynamic-slice_bitcast_fusion.1.wall_ref, bf16[2,384,768]{2,1,0:T(8,128)(2,1)} %constant.49.clone.span_ref, f32[48,192,384]{2,1,0:T(8,128)} %f_ref.27, ...), custom_call_target="tpu_custom_call", output_to_operand_aliasing={{0}: (7, {}), {1}: (8, {})} | custom-call | flops 6115295232 | bytes 19464192 | tf_op jit(solution)/shard_map/pallas_call | solution.py:243
  604.6 5.3 shard_map.118
  (143 shorter events, 204.8 us)
Async XLA Ops:
  136.4 48.9 %collective-permute-start.28 = (bf16[4,8,48,384]{3,2,1,0:T(8,128)(2,1)}, bf16[4,8,48,384]{3,2,1,0:T(8,128)(2,1)}, u32[]{:S(2)}, u32[]{:S(2)}) collective-permute-start(bf16[4,8,48,384]{3,2,1,0:T(8,128)(2,1)} %all-to-all-done.16.refs_4_), channel_id=1, source_target_pairs={{0,8},{2,10},{4,12},{6,14},{24,16},{26,18},{28,20},{30,22},{1,9},{... | collective-permute-start | bytes 3538952 | tf_op jit(solution)/shard_map/ppermute | solution.py:344
  145.3 45.7 %all-to-all-start.7 = ((bf16[4,8,48,384]{3,2,1,0:T(8,128)(2,1)}), bf16[4,8,48,384]{3,2,1,0:T(8,128)(2,1)S(1)}, u32[]{:S(2)}, u32[]{:S(2)}) async-start(bf16[4,8,48,384]{3,2,1,0:T(8,128)(2,1)} %get-tuple-element.53), calls=%async_computation.7 | async-start | bytes 2359296 | tf_op jit(solution)/shard_map/all_to_all | solution.py:341
  148.8 69.0 %collective-permute-start.20 = (bf16[4,8,48,384]{3,2,1,0:T(8,128)(2,1)}, bf16[4,8,48,384]{3,2,1,0:T(8,128)(2,1)}, u32[]{:S(2)}, u32[]{:S(2)}) collective-permute-start(bf16[4,8,48,384]{3,2,1,0:T(8,128)(2,1)} %all_to_all.91.refs_0_), channel_id=1, source_target_pairs={{0,8},{2,10},{4,12},{6,14},{24,16},{26,18},{28,20},{30,22},{1,9},{... | collective-permute-start | bytes 3538952 | tf_op jit(solution)/shard_map/ppermute | solution.py:342
  154.0 73.0 %collective-permute-start.21 = (bf16[4,8,48,384]{3,2,1,0:T(8,128)(2,1)}, bf16[4,8,48,384]{3,2,1,0:T(8,128)(2,1)}, u32[]{:S(2)}, u32[]{:S(2)}) collective-permute-start(bf16[4,8,48,384]{3,2,1,0:T(8,128)(2,1)} %all_to_all.91.refs_0_), channel_id=1, source_target_pairs={{8,16},{10,18},{12,20},{14,22},{16,8},{18,10},{20,12},{22,14},{9,1... | collective-permute-start | bytes 3538952 | tf_op jit(solution)/shard_map/ppermute | solution.py:343
  159.9 75.9 %collective-permute-start.23 = (bf16[4,8,48,384]{3,2,1,0:T(8,128)(2,1)}, bf16[4,8,48,384]{3,2,1,0:T(8,128)(2,1)}, u32[]{:S(2)}, u32[]{:S(2)}) collective-permute-start(bf16[4,8,48,384]{3,2,1,0:T(8,128)(2,1)} %all-to-all-done.13.refs_4_), channel_id=1, source_target_pairs={{0,8},{2,10},{4,12},{6,14},{24,16},{26,18},{28,20},{30,22},{1,9},{... | collective-permute-start | bytes 3538952 | tf_op jit(solution)/shard_map/ppermute | solution.py:344
  165.4 95.7 %collective-permute-start.15 = (bf16[4,8,48,384]{3,2,1,0:T(8,128)(2,1)}, bf16[4,8,48,384]{3,2,1,0:T(8,128)(2,1)}, u32[]{:S(2)}, u32[]{:S(2)}) collective-permute-start(bf16[4,8,48,384]{3,2,1,0:T(8,128)(2,1)} %all_to_all.92.refs_0_), channel_id=1, source_target_pairs={{0,8},{2,10},{4,12},{6,14},{24,16},{26,18},{28,20},{30,22},{1,9},{... | collective-permute-start | bytes 3538952 | tf_op jit(solution)/shard_map/ppermute | solution.py:342
  185.3 81.3 %collective-permute-start.27 = (bf16[4,8,48,384]{3,2,1,0:T(8,128)(2,1)}, bf16[4,8,48,384]{3,2,1,0:T(8,128)(2,1)}, u32[]{:S(2)}, u32[]{:S(2)}) collective-permute-start(bf16[4,8,48,384]{3,2,1,0:T(8,128)(2,1)} %collective-permute-done.25.refs_1_), channel_id=1, source_target_pairs={{8,16},{10,18},{12,20},{14,22},{16,8},{18,10},{20,12},{22,14},{9,1... | collective-permute-start | bytes 3538952 | tf_op jit(solution)/shard_map/ppermute | solution.py:345
  217.8 73.5 %collective-permute-start.22 = (bf16[4,8,48,384]{3,2,1,0:T(8,128)(2,1)}, bf16[4,8,48,384]{3,2,1,0:T(8,128)(2,1)}, u32[]{:S(2)}, u32[]{:S(2)}) collective-permute-start(bf16[4,8,48,384]{3,2,1,0:T(8,128)(2,1)} %collective-permute-done.20.refs_1_), channel_id=1, source_target_pairs={{8,16},{10,18},{12,20},{14,22},{16,8},{18,10},{20,12},{22,14},{9,1... | collective-permute-start | bytes 3538952 | tf_op jit(solution)/shard_map/ppermute | solution.py:345
  222.7 64.2 %all-to-all-start.4 = ((bf16[4,8,48,384]{3,2,1,0:T(8,128)(2,1)}), bf16[4,8,48,384]{3,2,1,0:T(8,128)(2,1)}, u32[]{:S(2)}, u32[]{:S(2)}) async-start(bf16[4,8,48,384]{3,2,1,0:T(8,128)(2,1)} %get-tuple-element.49), calls=%async_computation.4 | async-start | bytes 2359296 | tf_op jit(solution)/shard_map/all_to_all | solution.py:341
  227.1 88.3 %collective-permute-start.16 = (bf16[4,8,48,384]{3,2,1,0:T(8,128)(2,1)}, bf16[4,8,48,384]{3,2,1,0:T(8,128)(2,1)}, u32[]{:S(2)}, u32[]{:S(2)}) collective-permute-start(bf16[4,8,48,384]{3,2,1,0:T(8,128)(2,1)} %all_to_all.92.refs_0_), channel_id=1, source_target_pairs={{8,16},{10,18},{12,20},{14,22},{16,8},{18,10},{20,12},{22,14},{9,1... | collective-permute-start | bytes 3538952 | tf_op jit(solution)/shard_map/ppermute | solution.py:343
  235.9 80.4 %collective-permute-start.18 = (bf16[4,8,48,384]{3,2,1,0:T(8,128)(2,1)}, bf16[4,8,48,384]{3,2,1,0:T(8,128)(2,1)}, u32[]{:S(2)}, u32[]{:S(2)}) collective-permute-start(bf16[4,8,48,384]{3,2,1,0:T(8,128)(2,1)} %copy-done.9), channel_id=1, source_target_pairs={{0,8},{2,10},{4,12},{6,14},{24,16},{26,18},{28,20},{30,22},{1,9},{... | collective-permute-start | bytes 3538952 | tf_op jit(solution)/shard_map/ppermute | solution.py:344
  261.1 63.5 %collective-permute-start.10 = (bf16[4,8,48,384]{3,2,1,0:T(8,128)(2,1)S(1)}, bf16[4,8,48,384]{3,2,1,0:T(8,128)(2,1)}, u32[]{:S(2)}, u32[]{:S(2)}) collective-permute-start(bf16[4,8,48,384]{3,2,1,0:T(8,128)(2,1)S(1)} %all-to-all-done.6.refs_0_), channel_id=1, source_target_pairs={{0,8},{2,10},{4,12},{6,14},{24,16},{26,18},{28,20},{30,22},{1,9},{... | collective-permute-start | bytes 3538952 | tf_op jit(solution)/shard_map/ppermute | solution.py:342
  266.6 60.4 %collective-permute-start.17 = (bf16[4,8,48,384]{3,2,1,0:T(8,128)(2,1)}, bf16[4,8,48,384]{3,2,1,0:T(8,128)(2,1)}, u32[]{:S(2)}, u32[]{:S(2)}) collective-permute-start(bf16[4,8,48,384]{3,2,1,0:T(8,128)(2,1)} %collective-permute-done.15.refs_1_), channel_id=1, source_target_pairs={{8,16},{10,18},{12,20},{14,22},{16,8},{18,10},{20,12},{22,14},{9,1... | collective-permute-start | bytes 3538952 | tf_op jit(solution)/shard_map/ppermute | solution.py:345
  291.2 54.9 %collective-permute-start.29 = (bf16[4,8,48,384]{3,2,1,0:T(8,128)(2,1)}, bf16[4,8,48,384]{3,2,1,0:T(8,128)(2,1)}, u32[]{:S(2)}, u32[]{:S(2)}) collective-permute-start(bf16[4,8,48,384]{3,2,1,0:T(8,128)(2,1)} %get-tuple-element.66), channel_id=1, source_target_pairs={{8,0},{10,2},{12,4},{14,6},{16,24},{18,26},{20,28},{22,30},{9,1},{... | collective-permute-start | bytes 3538952 | tf_op jit(solution)/shard_map/ppermute | solution.py:347
  311.0 73.3 %all-to-all-start.1 = ((bf16[4,8,48,384]{3,2,1,0:T(8,128)(2,1)}), bf16[4,8,48,384]{3,2,1,0:T(8,128)(2,1)}, u32[]{:S(2)}, u32[]{:S(2)}) async-start(bf16[4,8,48,384]{3,2,1,0:T(8,128)(2,1)} %get-tuple-element.45), calls=%async_computation.1 | async-start | bytes 2359296 | tf_op jit(solution)/shard_map/all_to_all | solution.py:341
  324.6 51.5 %collective-permute-start.5 = (bf16[4,8,48,384]{3,2,1,0:T(8,128)(2,1)S(1)}, bf16[4,8,48,384]{3,2,1,0:T(8,128)(2,1)}, u32[]{:S(2)}, u32[]{:S(2)}) collective-permute-start(bf16[4,8,48,384]{3,2,1,0:T(8,128)(2,1)S(1)} %all-to-all-done.3.refs_0_), channel_id=1, source_target_pairs={{0,8},{2,10},{4,12},{6,14},{24,16},{26,18},{28,20},{30,22},{1,9},{... | collective-permute-start | bytes 3538952 | tf_op jit(solution)/shard_map/ppermute | solution.py:342
  326.9 54.7 %collective-permute-start.12 = (bf16[4,8,48,384]{3,2,1,0:T(8,128)(2,1)}, bf16[4,8,48,384]{3,2,1,0:T(8,128)(2,1)S(1)}, u32[]{:S(2)}, u32[]{:S(2)}) collective-permute-start(bf16[4,8,48,384]{3,2,1,0:T(8,128)(2,1)} %collective-permute-done.10.refs_1_), channel_id=1, source_target_pairs={{8,16},{10,18},{12,20},{14,22},{16,8},{18,10},{20,12},{22,14},{9,1... | collective-permute-start | bytes 3538952 | tf_op jit(solution)/shard_map/ppermute | solution.py:345
  346.1 60.7 %collective-permute-start.24 = (bf16[4,8,48,384]{3,2,1,0:T(8,128)(2,1)}, bf16[4,8,48,384]{3,2,1,0:T(8,128)(2,1)}, u32[]{:S(2)}, u32[]{:S(2)}) collective-permute-start(bf16[4,8,48,384]{3,2,1,0:T(8,128)(2,1)} %get-tuple-element.62), channel_id=1, source_target_pairs={{8,0},{10,2},{12,4},{14,6},{16,24},{18,26},{20,28},{22,30},{9,1},{... | collective-permute-start | bytes 3538952 | tf_op jit(solution)/shard_map/ppermute | solution.py:347
  349.9 60.7 %collective-permute-start.6 = (bf16[4,8,48,384]{3,2,1,0:T(8,128)(2,1)S(1)}, bf16[4,8,48,384]{3,2,1,0:T(8,128)(2,1)}, u32[]{:S(2)}, u32[]{:S(2)}) collective-permute-start(bf16[4,8,48,384]{3,2,1,0:T(8,128)(2,1)S(1)} %all-to-all-done.3.refs_0_), channel_id=1, source_target_pairs={{8,16},{10,18},{12,20},{14,22},{16,8},{18,10},{20,12},{22,14},{9,1... | collective-permute-start | bytes 3538952 | tf_op jit(solution)/shard_map/ppermute | solution.py:343
  351.6 60.5 %collective-permute-start.8 = (bf16[4,8,48,384]{3,2,1,0:T(8,128)(2,1)}, bf16[4,8,48,384]{3,2,1,0:T(8,128)(2,1)}, u32[]{:S(2)}, u32[]{:S(2)}) collective-permute-start(bf16[4,8,48,384]{3,2,1,0:T(8,128)(2,1)} %all-to-all-done.4.refs_4_), channel_id=1, source_target_pairs={{0,8},{2,10},{4,12},{6,14},{24,16},{26,18},{28,20},{30,22},{1,9},{... | collective-permute-start | bytes 3538952 | tf_op jit(solution)/shard_map/ppermute | solution.py:344
  376.1 49.9 %collective-permute-start = (bf16[4,8,48,384]{3,2,1,0:T(8,128)(2,1)}, bf16[4,8,48,384]{3,2,1,0:T(8,128)(2,1)}, u32[]{:S(2)}, u32[]{:S(2)}) collective-permute-start(bf16[4,8,48,384]{3,2,1,0:T(8,128)(2,1)} %all-to-all-done.refs_0_), channel_id=1, source_target_pairs={{0,8},{2,10},{4,12},{6,14},{24,16},{26,18},{28,20},{30,22},{1,9},{... | collective-permute-start | bytes 3538952 | tf_op jit(solution)/shard_map/ppermute | solution.py:342
  382.7 48.8 %collective-permute-start.7 = (bf16[4,8,48,384]{3,2,1,0:T(8,128)(2,1)}, bf16[4,8,48,384]{3,2,1,0:T(8,128)(2,1)}, u32[]{:S(2)}, u32[]{:S(2)}) collective-permute-start(bf16[4,8,48,384]{3,2,1,0:T(8,128)(2,1)} %collective-permute-done.5.refs_1_), channel_id=1, source_target_pairs={{8,16},{10,18},{12,20},{14,22},{16,8},{18,10},{20,12},{22,14},{9,1... | collective-permute-start | bytes 3538952 | tf_op jit(solution)/shard_map/ppermute | solution.py:345
  384.4 48.8 %all-to-all-start.17 = ((bf16[4,8,48,384]{3,2,1,0:T(8,128)(2,1)}), bf16[4,8,48,384]{3,2,1,0:T(8,128)(2,1)S(1)}, u32[]{:S(2)}, u32[]{:S(2)}) async-start(bf16[4,8,48,384]{3,2,1,0:T(8,128)(2,1)} %broadcast_select_fusion), calls=%async_computation.17 | async-start | bytes 2359296 | tf_op jit(solution)/shard_map/all_to_all | solution.py:349
  406.8 48.4 %collective-permute-start.19 = (bf16[4,8,48,384]{3,2,1,0:T(8,128)(2,1)}, bf16[4,8,48,384]{3,2,1,0:T(8,128)(2,1)S(1)}, u32[]{:S(2)}, u32[]{:S(2)}) collective-permute-start(bf16[4,8,48,384]{3,2,1,0:T(8,128)(2,1)} %get-tuple-element.58), channel_id=1, source_target_pairs={{8,0},{10,2},{12,4},{14,6},{16,24},{18,26},{20,28},{22,30},{9,1},{... | collective-permute-start | bytes 3538952 | tf_op jit(solution)/shard_map/ppermute | solution.py:347
  410.6 79.6 %collective-permute-start.33 = (bf16[12,192,384]{2,1,0:T(8,128)(2,1)}, bf16[12,192,384]{2,1,0:T(8,128)(2,1)}, u32[]{:S(2)}, u32[]{:S(2)}) collective-permute-start(bf16[12,192,384]{2,1,0:T(8,128)(2,1)} %shard_map.110), channel_id=1, source_target_pairs={{0,1},{1,0},{2,3},{3,2},{4,5},{5,4},{6,7},{7,6},{8,9},{9,8},{10,11... | collective-permute-start | bytes 5308424 | tf_op jit(solution)/shard_map/ppermute | solution.py:311
  412.1 45.6 %collective-permute-start.1 = (bf16[4,8,48,384]{3,2,1,0:T(8,128)(2,1)}, bf16[4,8,48,384]{3,2,1,0:T(8,128)(2,1)}, u32[]{:S(2)}, u32[]{:S(2)}) collective-permute-start(bf16[4,8,48,384]{3,2,1,0:T(8,128)(2,1)} %all-to-all-done.refs_0_), channel_id=1, source_target_pairs={{8,16},{10,18},{12,20},{14,22},{16,8},{18,10},{20,12},{22,14},{9,1... | collective-permute-start | bytes 3538952 | tf_op jit(solution)/shard_map/ppermute | solution.py:343
  457.7 59.7 %collective-permute-start.32 = (bf16[12,192,384]{2,1,0:T(8,128)(2,1)}, bf16[12,192,384]{2,1,0:T(8,128)(2,1)}, u32[]{:S(2)}, u32[]{:S(2)}) collective-permute-start(bf16[12,192,384]{2,1,0:T(8,128)(2,1)} %shard_map.109), channel_id=1, source_target_pairs={{0,1},{1,0},{2,3},{3,2},{4,5},{5,4},{6,7},{7,6},{8,9},{9,8},{10,11... | collective-permute-start | bytes 5308424 | tf_op jit(solution)/shard_map/ppermute | solution.py:311
  459.2 83.1 %collective-permute-start.31 = (bf16[12,192,384]{2,1,0:T(8,128)(2,1)}, bf16[12,192,384]{2,1,0:T(8,128)(2,1)}, u32[]{:S(2)}, u32[]{:S(2)}) collective-permute-start(bf16[12,192,384]{2,1,0:T(8,128)(2,1)} %shard_map.108), channel_id=1, source_target_pairs={{0,1},{1,0},{2,3},{3,2},{4,5},{5,4},{6,7},{7,6},{8,9},{9,8},{10,11... | collective-permute-start | bytes 5308424 | tf_op jit(solution)/shard_map/ppermute | solution.py:311
  459.8 51.7 %collective-permute-start.9 = (bf16[4,8,48,384]{3,2,1,0:T(8,128)(2,1)}, bf16[4,8,48,384]{3,2,1,0:T(8,128)(2,1)}, u32[]{:S(2)}, u32[]{:S(2)}) collective-permute-start(bf16[4,8,48,384]{3,2,1,0:T(8,128)(2,1)} %get-tuple-element.50), channel_id=1, source_target_pairs={{8,0},{10,2},{12,4},{14,6},{16,24},{18,26},{20,28},{22,30},{9,1},{... | collective-permute-start | bytes 3538952 | tf_op jit(solution)/shard_map/ppermute | solution.py:347
  486.2 88.6 %collective-permute-start.30 = (bf16[12,192,384]{2,1,0:T(8,128)(2,1)}, bf16[12,192,384]{2,1,0:T(8,128)(2,1)}, u32[]{:S(2)}, u32[]{:S(2)}) collective-permute-start(bf16[12,192,384]{2,1,0:T(8,128)(2,1)} %shard_map.107), channel_id=1, source_target_pairs={{0,1},{1,0},{2,3},{3,2},{4,5},{5,4},{6,7},{7,6},{8,9},{9,8},{10,11... | collective-permute-start | bytes 5308424 | tf_op jit(solution)/shard_map/ppermute | solution.py:311
  490.2 46.1 %collective-permute-start.4 = (bf16[4,8,48,384]{3,2,1,0:T(8,128)(2,1)}, bf16[4,8,48,384]{3,2,1,0:T(8,128)(2,1)}, u32[]{:S(2)}, u32[]{:S(2)}) collective-permute-start(bf16[4,8,48,384]{3,2,1,0:T(8,128)(2,1)} %get-tuple-element.46), channel_id=1, source_target_pairs={{8,0},{10,2},{12,4},{14,6},{16,24},{18,26},{20,28},{22,30},{9,1},{... | collective-permute-start | bytes 3538952 | tf_op jit(solution)/shard_map/ppermute | solution.py:347
  538.8 76.3 %all-to-all-start.2 = ((bf16[4,8,48,384]{3,2,1,0:T(8,128)(2,1)}), bf16[4,8,48,384]{3,2,1,0:T(8,128)(2,1)S(1)}, u32[]{:S(2)}, u32[]{:S(2)}) async-start(bf16[4,8,48,384]{3,2,1,0:T(8,128)(2,1)} %broadcast_select_fusion.5), calls=%async_computation.2 | async-start | bytes 2359296 | tf_op jit(solution)/shard_map/all_to_all | solution.py:349
  (37 other events, 1255.4 us)

commit v2 on v1

--- a/solution.py
+++ b/solution.py
@@ -103,11 +103,29 @@
     return pltpu.CompilerParams(vmem_limit_bytes=VMEM, **kw)
 
 
+COST = 1.0
+
+
 def cost(flops, moved):
-    return pl.CostEstimate(flops=int(flops), bytes_accessed=int(moved), transcendentals=0)
+    return pl.CostEstimate(flops=int(COST * flops), bytes_accessed=int(COST * moved), transcendentals=0)
+
+
+def launch(kernel, operands, in_specs, after, **kw):
+    count, extra = len(operands), len(after)
+
+    def run(*refs):
+        kernel(*refs[:count], *refs[count + extra:])
+
+    return pl.pallas_call(
+        run,
+        in_specs=list(in_specs) + [pl.BlockSpec(memory_space=pl.ANY)] * extra,
+        **kw,
+    )(*operands, *after)
 
 
 STEP = 16
+MARK = jax.ShapeDtypeStruct((8, 128), F32)
+MARK_BLOCK = pl.BlockSpec((8, 128), lambda i: (0, 0))
 
 
 def pack_kernel(f_ref, u_ref, g_ref, w_ref):
@@ -117,40 +135,44 @@
     w_ref[...] = u.astype(BF16).reshape(w_ref.shape)
 
 
-def pack(f, u, first_row, rows, shares):
+def pack(f, u, first_row, rows, shares, after):
     nx, ny, nz = f.shape
     each = rows // shares
     per = STEP // each
     out = jax.ShapeDtypeStruct((shares, each, nx, nz), BF16)
     base = first_row // STEP
-    return pl.pallas_call(
+    return launch(
         pack_kernel,
+        (f, u),
+        [pl.BlockSpec((nx, STEP, nz), lambda i: (0, base + i, 0))] * 2,
+        after,
         grid=(rows // STEP,),
-        in_specs=[pl.BlockSpec((nx, STEP, nz), lambda i: (0, base + i, 0))] * 2,
         out_specs=[pl.BlockSpec((per, each, nx, nz), lambda i: (i, 0, 0, 0))] * 2,
         out_shape=[out, out],
         compiler_params=params(),
         cost_estimate=cost(0, rows * nx * nz * 10),
-    )(f, u)
+    )
 
 
 def code_kernel(f_ref, h_ref):
     h_ref[...] = encode_scalar(f_ref[...]).astype(BF16)
 
 
-def code(f, first, planes):
+def code(f, first, planes, after):
     _, ny, nz = f.shape
     step = 4
     base = first // step
-    return pl.pallas_call(
+    return launch(
         code_kernel,
+        (f,),
+        [pl.BlockSpec((step, ny, nz), lambda i: (base + i, 0, 0))],
+        after,
         grid=(planes // step,),
-        in_specs=[pl.BlockSpec((step, ny, nz), lambda i: (base + i, 0, 0))],
         out_specs=pl.BlockSpec((step, ny, nz), lambda i: (i, 0, 0)),
         out_shape=jax.ShapeDtypeStruct((planes, ny, nz), BF16),
         compiler_params=params(),
         cost_estimate=cost(0, planes * ny * nz * 6),
-    )(f)
+    )
 
 
 def stream_kernel(n_in, n_out, rate, table_ref, *refs):
@@ -183,7 +205,7 @@
             start += tall
 
 
-def stream(table, fields, speeds, rate):
+def stream(table, fields, speeds, rate, after):
     parts, rows, nx, nz = fields[0].shape
     n_in, n_out = len(fields), len(speeds)
     step = 2 if rows % 2 == 0 else 1
@@ -191,19 +213,22 @@
     whole = pl.BlockSpec(table.shape, lambda i: (0, 0, 0, 0), pipeline_mode=pl.Buffered(1))
     points = table.shape[2] * table.shape[3]
     moved = 2 * (n_in + 2 * n_out) * parts * rows * nx * nz
-    return pl.pallas_call(
+    return launch(
         functools.partial(stream_kernel, n_in, n_out, rate),
+        (table, *fields, *speeds),
+        [whole] + [block] * (n_in + n_out),
+        after,
         grid=(rows // step,),
-        in_specs=[whole] + [block] * (n_in + n_out),
         out_specs=[block] * n_out,
         out_shape=[jax.ShapeDtypeStruct(fields[0].shape, BF16)] * n_out,
         compiler_params=params(),
         cost_estimate=cost(12 * points * rows * nz, moved),
-    )(table, *fields, *speeds)
+    )
 
 
 def local_kernel(wall_ref, span_ref, f_ref, h_ref, v_ref, w_ref, p_ref, *refs):
-    next_ref, tend_ref = refs[-2:]
+    next_ref, tend_ref, mark_ref = refs[-3:]
+    mark_ref[...] = jnp.zeros_like(mark_ref)
     planes, ny, nz = f_ref.shape
     own = f_ref[...]
     other = decode_scalar(h_ref[...].astype(F32))
@@ -231,7 +256,7 @@
         next_ref[x] = own[x] + GAMMA_RK * tendency + ZETA_RK * p_ref[x]
 
 
-def local(wall, span, f, h, v, w, prev, first, held):
+def local(wall, span, f, h, v, w, prev, first, held, after):
     nx, ny, nz = f.shape
     planes = h.shape[0]
     step = 2
@@ -240,21 +265,24 @@
     table = lambda t: pl.BlockSpec(t.shape, lambda i: (0, 0, 0), pipeline_mode=pl.Buffered(1))
     out = jax.ShapeDtypeStruct(f.shape, F32)
     keep = pl.BlockSpec(memory_space=pl.ANY)
-    return pl.pallas_call(
+    return launch(
         local_kernel,
+        (wall, span, f, h, v, w, prev, *held),
+        [table(wall), table(span), block,
+         pl.BlockSpec((step, ny, nz), lambda i: (i, 0, 0)), block, block, block]
+        + [keep] * len(held),
+        after,
         grid=(planes // step,),
-        in_specs=[table(wall), table(span), block,
-                  pl.BlockSpec((step, ny, nz), lambda i: (i, 0, 0)), block, block, block]
-        + [keep] * len(held),
-        out_specs=[block, block],
-        out_shape=[out, out],
+        out_specs=[block, block, MARK_BLOCK],
+        out_shape=[out, out, MARK],
         input_output_aliases={7 + k: k for k in range(len(held))},
         compiler_params=params(),
         cost_estimate=cost(6 * planes * ny * nz * (2 * ny + 2 * nz), planes * ny * nz * 22),
-    )(wall, span, f, h, v, w, prev, *held)
-
-
-def merge_kernel(rate, s_ref, next_ref, tend_ref, next_out, tend_out):
+    )
+
+
+def merge_kernel(rate, s_ref, next_ref, tend_ref, next_out, tend_out, mark_ref):
+    mark_ref[...] = jnp.zeros_like(mark_ref)
     nx, step, nz = next_ref.shape
     coded = jnp.swapaxes(s_ref[...].astype(F32).reshape(step, nx, nz), 0, 1)
     add = DT_STEP * decode_stream(coded, rate)
@@ -262,28 +290,33 @@
     next_out[...] = next_ref[...] + GAMMA_RK * add
 
 
-def merge(s, held, first_row, rate):
+def merge(s, held, first_row, rate, after):
     nx, ny, nz = held[0].shape
     shares, each = s.shape[:2]
     per = STEP // each
     base = first_row // STEP
     block = pl.BlockSpec((nx, STEP, nz), lambda i: (0, base + i, 0))
     out = jax.ShapeDtypeStruct(held[0].shape, F32)
-    return pl.pallas_call(
+    return launch(
         functools.partial(merge_kernel, rate),
+        (s, *held),
+        [pl.BlockSpec((per, each, nx, nz), lambda i: (i, 0, 0, 0)), block, block],
+        after,
         grid=(shares * each // STEP,),
-        in_specs=[pl.BlockSpec((per, each, nx, nz), lambda i: (i, 0, 0, 0)), block, block],
-        out_specs=[block, block],
-        out_shape=[out, out],
+        out_specs=[block, block, MARK_BLOCK],
+        out_shape=[out, out, MARK],
         input_output_aliases={1: 0, 2: 1},
         compiler_params=params(),
         cost_estimate=cost(0, shares * each * nx * nz * 18),
-    )(s, *held)
+    )
 
 
 CHUNKS = (32,) * 6
 PIECES = 4
-PLAIN = False
+ORDER = (
+    "P0", "Y0", "P1", "Y1", "Y2", "Y3", "P2", "L0", "X0", "P3", "L1", "X1", "P4", "L2", "X2",
+    "P5", "L3", "X3", "M0", "X4", "M1", "M2", "X5", "M3", "M4", "M5",
+)
 
 
 def body(px, pz, f, prev, u, v, w):
@@ -305,55 +338,78 @@
         wall_all.append(two_terms(np.concatenate([own, other], axis=1)))
     wall = lax.dynamic_index_in_dim(jnp.asarray(np.stack(wall_all)), mine, 0, keepdims=False)
 
+    ring = px // 4
+    quarter = nx * ring
+    variants = []
+    for order in ((1, 0, 2, 3), (2, 3, 1, 0)):
+        pick = lambda m: np.concatenate(
+            [np.concatenate([m[o * quarter:(o + 1) * quarter, q * quarter:(q + 1) * quarter] for q in order], axis=1)
+             for o in order[:2]], axis=0)
+        variants.append(np.stack([two_terms(pick(k_first)), two_terms(pick(k_second))], axis=1))
+    level = lax.axis_index("px") // ring
+    table = lax.dynamic_index_in_dim(jnp.asarray(np.stack(variants)), level // 2, 0, keepdims=False)
+    outer = (level == 0) | (level == 3)
+    groups = [[l * ring + r for r in range(ring)] for l in range(4)]
+    hop = lambda pairs: [(a * ring + r, b * ring + r) for a, b in pairs for r in range(ring)]
+    inward, across, outward = hop([(0, 1), (3, 2)]), hop([(1, 2), (2, 1)]), hop([(1, 0), (2, 3)])
     planes = nx // PIECES
-    theirs = []
-    for p in range(PIECES):
-        theirs.append(lax.ppermute(code(f, p * planes, planes), "pz", [(0, 1), (1, 0)]))
-
-    starts = np.concatenate([[0], np.cumsum(CHUNKS)])[:-1]
-    streams = []
-    if PLAIN:
-        table = jnp.asarray(np.stack([two_terms(k_first), two_terms(k_second)], axis=1))
-        for at, rows in zip(starts, CHUNKS):
-            g, ut = pack(f, u, int(at), rows, px)
-            g = lax.all_to_all(g, "px", 0, 0, tiled=True)
-            ut = lax.all_to_all(ut, "px", 0, 0, tiled=True)
-            (s,) = stream(table, [g], [ut], rate)
-            streams.append(lax.all_to_all(s, "px", 0, 0, tiled=True))
-    else:
-        ring = px // 4
-        quarter = nx * ring
-        variants = []
-        for order in ((1, 0, 2, 3), (2, 3, 1, 0)):
-            pick = lambda m: np.concatenate(
-                [np.concatenate([m[o * quarter:(o + 1) * quarter, q * quarter:(q + 1) * quarter] for q in order], axis=1)
-                 for o in order[:2]], axis=0)
-            variants.append(np.stack([two_terms(pick(k_first)), two_terms(pick(k_second))], axis=1))
-        level = lax.axis_index("px") // ring
-        table = lax.dynamic_index_in_dim(jnp.asarray(np.stack(variants)), level // 2, 0, keepdims=False)
-        outer = (level == 0) | (level == 3)
-        groups = [[l * ring + r for r in range(ring)] for l in range(4)]
-        hop = lambda pairs: [(a * ring + r, b * ring + r) for a, b in pairs for r in range(ring)]
-        inward, across, outward = hop([(0, 1), (3, 2)]), hop([(1, 2), (2, 1)]), hop([(1, 0), (2, 3)])
-        for at, rows in zip(starts, CHUNKS):
-            g, ut = pack(f, u, int(at), rows, ring)
-            g = lax.all_to_all(g, "px", 0, 0, axis_index_groups=groups, tiled=True)
-            ut = lax.all_to_all(ut, "px", 0, 0, axis_index_groups=groups, tiled=True)
-            near = lax.ppermute(g, "px", inward)
-            far = lax.ppermute(g, "px", across)
-            near_u = lax.ppermute(ut, "px", inward)
-            far_near = lax.ppermute(near, "px", across)
-            s_own, s_near = stream(table, [g, near, far, far_near], [ut, near_u], rate)
-            got = lax.ppermute(s_near, "px", outward)
-            s = jnp.where(outer, got, s_own)
-            streams.append(lax.all_to_all(s, "px", 0, 0, axis_index_groups=groups, tiled=True))
+    starts = [int(x) for x in np.concatenate([[0], np.cumsum(CHUNKS)])]
+
+    made = {}
+    last = ()
+
+    def exchange(x):
+        return lax.all_to_all(x, "px", 0, 0, axis_index_groups=groups, tiled=True)
+
+    def after(names):
+        return tuple(last) + tuple(made[n] for n in names.split())
+
+    def send(name, x, pairs, axis="px"):
+        with jax.named_scope("send_" + name):
+            made[name] = lax.ppermute(x, axis, pairs)
+        return made[name]
+
+    def share(name, x):
+        with jax.named_scope("share_" + name):
+            made[name] = lax.all_to_all(x, "px", 0, 0, axis_index_groups=groups, tiled=True)
+        return made[name]
 
     held = ()
-    for p in range(PIECES):
-        held = tuple(local(wall, span, f, theirs[p], v, w, prev, p * planes, held))
-    for at, s in zip(starts, streams):
-        held = tuple(merge(s, held, int(at), rate))
-    return held
+    for word in ORDER:
+        name, _, waits = word.partition(":")
+        kind, c = name[0], int(name[1:])
+        with jax.named_scope("kernel_" + name):
+            if kind == "P":
+                g, ut = pack(f, u, starts[c], CHUNKS[c], ring, after(waits))
+                last = (g,)
+            elif kind == "Y":
+                h = code(f, c * planes, planes, after(waits))
+                last = (h,)
+            elif kind == "L":
+                *held, mark = local(wall, span, f, made[f"y{c}"], v, w, prev, c * planes, held, after(waits))
+                last = (mark,)
+            elif kind == "X":
+                fields = [made[f"{k}{c}"] for k in "gnab"]
+                speeds = [made[f"{k}{c}"] for k in "uv"]
+                s_own, s_near = stream(table, fields, speeds, rate, after(waits))
+                last = (s_own,)
+            else:
+                *held, mark = merge(made[f"r{c}"], held, starts[c], rate, after(waits))
+                last = (mark,)
+        if kind == "P":
+            g = share(f"g{c}", g)
+            ut = share(f"u{c}", ut)
+            near = send(f"n{c}", g, inward)
+            send(f"a{c}", g, across)
+            send(f"v{c}", ut, inward)
+            send(f"b{c}", near, across)
+        elif kind == "Y":
+            send(f"y{c}", h, [(0, 1), (1, 0)], "pz")
+        elif kind == "X":
+            got = send(f"o{c}", s_near, outward)
+            made[f"s{c}"] = s = jnp.where(outer, got, s_own)
+            share(f"r{c}", s)
+    return tuple(held)
 
 
 def plain_wall(points):

time: 632 us -> 536 us (0.85)
  waiting for transfers between devices: 150 us -> 77.7 us
  blocking collectives: 60.5 us -> 20.8 us
  starting transfers between devices: 149 us -> 166 us
    ppermute x34, waiting for transfers between devices: 108 us -> 48.4 us  [send(): made[name] = lax.ppermute(x, axis, pairs)]
    all_to_all x3 -> x1, blocking collectives: 60.5 us -> 20.8 us  [share(): lax.all_to_all(x, 'px', 0, 0, axis_index_groups=groups, tiled=True)]
    all_to_all x15 -> x17, waiting for transfers between devices: 41.8 us -> 29.3 us  [share(): lax.all_to_all(x, 'px', 0, 0, axis_index_groups=groups, tiled=True)]
    all_to_all x15 -> x17, starting transfers between devices: 57.3 us -> 68.4 us  [share(): lax.all_to_all(x, 'px', 0, 0, axis_index_groups=groups, tiled=True)]
    ppermute x34, starting transfers between devices: 91.5 us -> 97.8 us  [send(): made[name] = lax.ppermute(x, axis, pairs)]
  transfers between devices with their start and end apart: 49 -> 51, of which waited for: 14 -> 11; matrix products, arithmetic and copies ran while one was open for 3% -> 3% of each run, Pallas kernels for 37% -> 44%
where the time goes in v2:
time: 536 us; the launch traced here: 527 us
  Pallas kernels  240 us (45%)
  starting transfers between devices  166 us (31%)
  waiting for transfers between devices  77.7 us (14%)
  blocking collectives  20.8 us (4%)
  other arithmetic  13.3 us (2%)
  local copies, waits for them, and re-layouts  8.31 us (2%)
    pallas_call x26, Pallas kernels, launch(): pl.pallas_call(run, in_specs=list(in_specs) + [pl.BlockSpec(memory_space=...  240 us
    ppermute x34, starting transfers between devices, send(): made[name] = lax.ppermute(x, axis, pairs)  97.8 us
    all_to_all x17, starting transfers between devices, share(): lax.all_to_all(x, 'px', 0, 0, axis_index_groups=groups, tiled=True)  68.4 us
    ppermute x34, waiting for transfers between devices, send(): made[name] = lax.ppermute(x, axis, pairs)  48.4 us
    all_to_all x17, waiting for transfers between devices, share(): lax.all_to_all(x, 'px', 0, 0, axis_index_groups=groups, tiled=True)  29.3 us
    all_to_all x1, blocking collectives, share(): lax.all_to_all(x, 'px', 0, 0, axis_index_groups=groups, tiled=True)  20.8 us
    select_n x6, other arithmetic, body(): made[f's{c}'] = s = jnp.where(outer, got, s_own)  13.3 us
  transfers between devices with their start and end apart: 51, of which 11 were waited for; matrix products, arithmetic and copies ran while one was open for 3% of the time, Pallas kernels for 44%

profile of v2, /device:TPU:0, one launch (start us, length us, event | category | flops | bytes accessed | tf_op | source)
XLA Modules:
  0.0 527.4 jit_solution(6263839477862998731)
XLA Ops:
  4.5 20.8 %all_to_all.90.refs_1_ = bf16[4,8,48,384]{3,2,1,0:T(8,128)(2,1)} all-to-all(bf16[4,8,48,384]{3,2,1,0:T(8,128)(2,1)} %get-tuple-element.55.refs_1_), channel_id=1, replica_groups={{0,2,4,6},{8,10,12,14},{16,18,20,22},{24,26,28,30},{1,3,5,7},{9,11,13,1..., dimensions={0} | all-to-all | bytes 2359296 | tf_op jit(solution)/shard_map/share_g0/all_to_all | solution.py:374
  37.9 7.7 %all-to-all-done.3.refs_5_ = bf16[4,8,48,384]{3,2,1,0:T(8,128)(2,1)} async-done(((bf16[4,8,48,384]{3,2,1,0:T(8,128)(2,1)}), bf16[4,8,48,384]{3,2,1,0:T(8,128)(2,1)}, u32[]{:S(2)}, u32[]{:S(2)}) %all-to-all-start.3) | async-done | bytes 1179680 | tf_op jit(solution)/shard_map/share_u0/all_to_all | solution.py:374
  50.0 5.3 %collective-permute-start.7 = (bf16[4,8,48,384]{3,2,1,0:T(8,128)(2,1)}, bf16[4,8,48,384]{3,2,1,0:T(8,128)(2,1)}, u32[]{:S(2)}, u32[]{:S(2)}) collective-permute-start(bf16[4,8,48,384]{3,2,1,0:T(8,128)(2,1)} %all_to_all.90.refs_1_), channel_id=1, source_target_pairs={{0,8},{2,10},{4,12},{6,14},{24,16},{26,18},{28,20},{30,22},{1,9},{... | collective-permute-start | bytes 3538952 | tf_op jit(solution)/shard_map/send_n0/ppermute | solution.py:369
  56.8 9.1 %all-to-all-done.4.refs_1_ = bf16[4,8,48,384]{3,2,1,0:T(8,128)(2,1)} async-done(((bf16[4,8,48,384]{3,2,1,0:T(8,128)(2,1)}), bf16[4,8,48,384]{3,2,1,0:T(8,128)(2,1)}, u32[]{:S(2)}, u32[]{:S(2)}) %all-to-all-start.4) | async-done | bytes 1179680 | tf_op jit(solution)/shard_map/share_g1/all_to_all | solution.py:374
  72.0 7.1 %collective-permute-start.10 = (bf16[4,8,48,384]{3,2,1,0:T(8,128)(2,1)}, bf16[4,8,48,384]{3,2,1,0:T(8,128)(2,1)}, u32[]{:S(2)}, u32[]{:S(2)}) collective-permute-start(bf16[4,8,48,384]{3,2,1,0:T(8,128)(2,1)} %all-to-all-done.3.refs_5_), channel_id=1, source_target_pairs={{0,8},{2,10},{4,12},{6,14},{24,16},{26,18},{28,20},{30,22},{1,9},{... | collective-permute-start | bytes 3538952 | tf_op jit(solution)/shard_map/send_v0/ppermute | solution.py:369
  110.3 14.1 %kernel_L0.1 = (f32[48,192,384]{2,1,0:T(8,128)}, f32[48,192,384]{2,1,0:T(8,128)}, f32[8,128]{1,0:T(8,128)}) custom-call(bf16[2,192,384]{2,1,0:T(8,128)(2,1)} %dynamic-slice_bitcast_fusion.1.refs_0_, bf16[2,384,768]{2,1,0:T(8,128)(2,1)} %constant.49.clone.refs_1_, f32[48,192,384]{2,1,0:T(8,128)} %refs_2_.7, ...), custom_call_target="tpu_custom_call" | custom-call | flops 6115295232 | bytes 19464192 | tf_op jit(solution)/shard_map/kernel_L0/pallas_call | solution.py:119
  130.4 7.3 %collective-permute-start.14 = (bf16[4,8,48,384]{3,2,1,0:T(8,128)(2,1)}, bf16[4,8,48,384]{3,2,1,0:T(8,128)(2,1)}, u32[]{:S(2)}, u32[]{:S(2)}) collective-permute-start(bf16[4,8,48,384]{3,2,1,0:T(8,128)(2,1)} %all-to-all-done.5.refs_5_), channel_id=1, source_target_pairs={{0,8},{2,10},{4,12},{6,14},{24,16},{26,18},{28,20},{30,22},{1,9},{... | collective-permute-start | bytes 3538952 | tf_op jit(solution)/shard_map/send_v1/ppermute | solution.py:369
  142.0 18.4 %kernel_X0.1 = (bf16[4,8,48,384]{3,2,1,0:T(8,128)(2,1)}, bf16[4,8,48,384]{3,2,1,0:T(8,128)(2,1)}) custom-call(bf16[2,2,384,768]{3,2,1,0:T(8,128)(2,1)} %dynamic-slice_bitcast_fusion.refs_0_, bf16[4,8,48,384]{3,2,1,0:T(8,128)(2,1)} %all_to_all.90.refs_1_, bf16[4,8,48,384]{3,2,1,0:T(8,128)(2,1)} %collective-permute-done.7.refs_2_, ...), custom_call_target="tpu_custom_call" | custom-call | flops 10871635968 | bytes 9437184 | tf_op jit(solution)/shard_map/kernel_X0/pallas_call | solution.py:119
  169.4 14.0 %kernel_L1.1 = (f32[48,192,384]{2,1,0:T(8,128)}, f32[48,192,384]{2,1,0:T(8,128)}, f32[8,128]{1,0:T(8,128)}) custom-call(bf16[2,192,384]{2,1,0:T(8,128)(2,1)} %dynamic-slice_bitcast_fusion.1.refs_0_, bf16[2,384,768]{2,1,0:T(8,128)(2,1)} %constant.49.clone.refs_1_, f32[48,192,384]{2,1,0:T(8,128)} %refs_2_.7, ...), custom_call_target="tpu_custom_call", output_to_operand_aliasing={{0}: (7, {}), {1}: (8, {})} | custom-call | flops 6115295232 | bytes 19464192 | tf_op jit(solution)/shard_map/kernel_L1/pallas_call | solution.py:119
  193.8 18.5 %kernel_X1.1 = (bf16[4,8,48,384]{3,2,1,0:T(8,128)(2,1)}, bf16[4,8,48,384]{3,2,1,0:T(8,128)(2,1)}) custom-call(bf16[2,2,384,768]{3,2,1,0:T(8,128)(2,1)} %dynamic-slice_bitcast_fusion.refs_0_, bf16[4,8,48,384]{3,2,1,0:T(8,128)(2,1)} %all-to-all-done.4.refs_1_, bf16[4,8,48,384]{3,2,1,0:T(8,128)(2,1)} %collective-permute-done.11.refs_2_, ...), custom_call_target="tpu_custom_call" | custom-call | flops 10871635968 | bytes 9437184 | tf_op jit(solution)/shard_map/kernel_X1/pallas_call | solution.py:119
  217.2 4.9 all-to-all-start.13
  223.2 14.0 %kernel_L2.1 = (f32[48,192,384]{2,1,0:T(8,128)}, f32[48,192,384]{2,1,0:T(8,128)}, f32[8,128]{1,0:T(8,128)}) custom-call(bf16[2,192,384]{2,1,0:T(8,128)(2,1)} %dynamic-slice_bitcast_fusion.1.refs_0_, bf16[2,384,768]{2,1,0:T(8,128)(2,1)} %constant.49.clone.refs_1_, f32[48,192,384]{2,1,0:T(8,128)} %refs_2_.7, ...), custom_call_target="tpu_custom_call", output_to_operand_aliasing={{0}: (7, {}), {1}: (8, {})} | custom-call | flops 6115295232 | bytes 19464192 | tf_op jit(solution)/shard_map/kernel_L2/pallas_call | solution.py:119
  241.6 18.4 %kernel_X2.1 = (bf16[4,8,48,384]{3,2,1,0:T(8,128)(2,1)}, bf16[4,8,48,384]{3,2,1,0:T(8,128)(2,1)}) custom-call(bf16[2,2,384,768]{3,2,1,0:T(8,128)(2,1)} %dynamic-slice_bitcast_fusion.refs_0_, bf16[4,8,48,384]{3,2,1,0:T(8,128)(2,1)} %all-to-all-done.refs_1_, bf16[4,8,48,384]{3,2,1,0:T(8,128)(2,1)} %collective-permute-done.refs_2_, ...), custom_call_target="tpu_custom_call" | custom-call | flops 10871635968 | bytes 9437184 | tf_op jit(solution)/shard_map/kernel_X2/pallas_call | solution.py:119
  270.6 8.2 %collective-permute-start.23 = (bf16[4,8,48,384]{3,2,1,0:T(8,128)(2,1)}, bf16[4,8,48,384]{3,2,1,0:T(8,128)(2,1)}, u32[]{:S(2)}, u32[]{:S(2)}) collective-permute-start(bf16[4,8,48,384]{3,2,1,0:T(8,128)(2,1)} %all-to-all-done.11.refs_1_), channel_id=1, source_target_pairs={{0,8},{2,10},{4,12},{6,14},{24,16},{26,18},{28,20},{30,22},{1,9},{... | collective-permute-start | bytes 3538952 | tf_op jit(solution)/shard_map/send_n3/ppermute | solution.py:369
  278.9 6.4 %all-to-all-done.6.refs_1_ = bf16[4,8,48,384]{3,2,1,0:T(8,128)(2,1)} async-done(((bf16[4,8,48,384]{3,2,1,0:T(8,128)(2,1)}), bf16[4,8,48,384]{3,2,1,0:T(8,128)(2,1)}, u32[]{:S(2)}, u32[]{:S(2)}) %all-to-all-start.6) | async-done | bytes 1179680 | tf_op jit(solution)/shard_map/share_g5/all_to_all | solution.py:374
  292.7 9.0 %collective-permute-start.26 = (bf16[4,8,48,384]{3,2,1,0:T(8,128)(2,1)}, bf16[4,8,48,384]{3,2,1,0:T(8,128)(2,1)}, u32[]{:S(2)}, u32[]{:S(2)}) collective-permute-start(bf16[4,8,48,384]{3,2,1,0:T(8,128)(2,1)} %copy-done.18), channel_id=1, source_target_pairs={{0,8},{2,10},{4,12},{6,14},{24,16},{26,18},{28,20},{30,22},{1,9},{... | collective-permute-start | bytes 3538952 | tf_op jit(solution)/shard_map/send_v3/ppermute | solution.py:369
  312.1 14.1 %kernel_L3.1 = (f32[48,192,384]{2,1,0:T(8,128)}, f32[48,192,384]{2,1,0:T(8,128)}, f32[8,128]{1,0:T(8,128)}) custom-call(bf16[2,192,384]{2,1,0:T(8,128)(2,1)} %dynamic-slice_bitcast_fusion.1.refs_0_, bf16[2,384,768]{2,1,0:T(8,128)(2,1)} %constant.49.clone.refs_1_, f32[48,192,384]{2,1,0:T(8,128)} %refs_2_.7, ...), custom_call_target="tpu_custom_call", output_to_operand_aliasing={{0}: (7, {}), {1}: (8, {})} | custom-call | flops 6115295232 | bytes 19464192 | tf_op jit(solution)/shard_map/kernel_L3/pallas_call | solution.py:119
  332.6 6.0 %collective-permute-start.30 = (bf16[4,8,48,384]{3,2,1,0:T(8,128)(2,1)S(1)}, bf16[4,8,48,384]{3,2,1,0:T(8,128)(2,1)}, u32[]{:S(2)}, u32[]{:S(2)}) collective-permute-start(bf16[4,8,48,384]{3,2,1,0:T(8,128)(2,1)S(1)} %copy-done.17), channel_id=1, source_target_pairs={{0,8},{2,10},{4,12},{6,14},{24,16},{26,18},{28,20},{30,22},{1,9},{... | collective-permute-start | bytes 3538952 | tf_op jit(solution)/shard_map/send_v4/ppermute | solution.py:369
  338.6 16.3 %collective-permute-done.27.refs_2_ = bf16[4,8,48,384]{3,2,1,0:T(8,128)(2,1)} collective-permute-done((bf16[4,8,48,384]{3,2,1,0:T(8,128)(2,1)}, bf16[4,8,48,384]{3,2,1,0:T(8,128)(2,1)}, u32[]{:S(2)}, u32[]{:S(2)}) %collective-permute-start.27) | collective-permute-done | bytes 1179680 | tf_op jit(solution)/shard_map/send_n4/ppermute | solution.py:369
  354.9 5.4 %collective-permute-start.15 = (bf16[4,8,48,384]{3,2,1,0:T(8,128)(2,1)}, bf16[4,8,48,384]{3,2,1,0:T(8,128)(2,1)}, u32[]{:S(2)}, u32[]{:S(2)}) collective-permute-start(bf16[4,8,48,384]{3,2,1,0:T(8,128)(2,1)} %all-to-all-done.6.refs_1_), channel_id=1, source_target_pairs={{0,8},{2,10},{4,12},{6,14},{24,16},{26,18},{28,20},{30,22},{1,9},{... | collective-permute-start | bytes 3538952 | tf_op jit(solution)/shard_map/send_n5/ppermute | solution.py:369
  365.9 18.5 %kernel_X3.1 = (bf16[4,8,48,384]{3,2,1,0:T(8,128)(2,1)}, bf16[4,8,48,384]{3,2,1,0:T(8,128)(2,1)}) custom-call(bf16[2,2,384,768]{3,2,1,0:T(8,128)(2,1)} %dynamic-slice_bitcast_fusion.refs_0_, bf16[4,8,48,384]{3,2,1,0:T(8,128)(2,1)} %all-to-all-done.11.refs_1_, bf16[4,8,48,384]{3,2,1,0:T(8,128)(2,1)} %collective-permute-done.23.refs_2_, ...), custom_call_target="tpu_custom_call" | custom-call | flops 10871635968 | bytes 9437184 | tf_op jit(solution)/shard_map/kernel_X3/pallas_call | solution.py:119
  388.1 5.2 kernel_M0.1
  395.1 6.0 %collective-permute-start.18 = (bf16[4,8,48,384]{3,2,1,0:T(8,128)(2,1)}, bf16[4,8,48,384]{3,2,1,0:T(8,128)(2,1)}, u32[]{:S(2)}, u32[]{:S(2)}) collective-permute-start(bf16[4,8,48,384]{3,2,1,0:T(8,128)(2,1)} %all-to-all-done.7.refs_5_), channel_id=1, source_target_pairs={{0,8},{2,10},{4,12},{6,14},{24,16},{26,18},{28,20},{30,22},{1,9},{... | collective-permute-start | bytes 3538952 | tf_op jit(solution)/shard_map/send_v5/ppermute | solution.py:369
  407.2 18.5 %kernel_X4.1 = (bf16[4,8,48,384]{3,2,1,0:T(8,128)(2,1)}, bf16[4,8,48,384]{3,2,1,0:T(8,128)(2,1)}) custom-call(bf16[2,2,384,768]{3,2,1,0:T(8,128)(2,1)} %dynamic-slice_bitcast_fusion.refs_0_, bf16[4,8,48,384]{3,2,1,0:T(8,128)(2,1)} %all-to-all-done.13.refs_1_, bf16[4,8,48,384]{3,2,1,0:T(8,128)(2,1)} %collective-permute-done.27.refs_2_, ...), custom_call_target="tpu_custom_call" | custom-call | flops 10871635968 | bytes 9437184 | tf_op jit(solution)/shard_map/kernel_X4/pallas_call | solution.py:119
  427.0 5.3 kernel_M1.1
  433.4 5.3 %kernel_M2.1 = (f32[48,192,384]{2,1,0:T(8,128)}, f32[48,192,384]{2,1,0:T(8,128)}, f32[8,128]{1,0:T(8,128)}) custom-call(bf16[4,8,48,384]{3,2,1,0:T(8,128)(2,1)} %copy-done.4, f32[48,192,384]{2,1,0:T(8,128)} %get-tuple-element.90.refs_1_, f32[48,192,384]{2,1,0:T(8,128)} %get-tuple-element.91.refs_2_, ...), custom_call_target="tpu_custom_call", output_to_operand_aliasing={{0}: (1, {}), {1}: (2, {})} | custom-call | bytes 10616832 | tf_op jit(solution)/shard_map/kernel_M2/pallas_call | solution.py:119
  444.9 18.5 %kernel_X5.1 = (bf16[4,8,48,384]{3,2,1,0:T(8,128)(2,1)}, bf16[4,8,48,384]{3,2,1,0:T(8,128)(2,1)}) custom-call(bf16[2,2,384,768]{3,2,1,0:T(8,128)(2,1)} %dynamic-slice_bitcast_fusion.refs_0_, bf16[4,8,48,384]{3,2,1,0:T(8,128)(2,1)} %all-to-all-done.6.refs_1_, bf16[4,8,48,384]{3,2,1,0:T(8,128)(2,1)} %collective-permute-done.15.refs_2_, ...), custom_call_target="tpu_custom_call" | custom-call | flops 10871635968 | bytes 9437184 | tf_op jit(solution)/shard_map/kernel_X5/pallas_call | solution.py:119
  469.7 29.4 %collective-permute-done.31 = bf16[4,8,48,384]{3,2,1,0:T(8,128)(2,1)} collective-permute-done((bf16[4,8,48,384]{3,2,1,0:T(8,128)(2,1)}, bf16[4,8,48,384]{3,2,1,0:T(8,128)(2,1)}, u32[]{:S(2)}, u32[]{:S(2)}) %collective-permute-start.31) | collective-permute-done | bytes 1179680 | tf_op jit(solution)/shard_map/send_o5/ppermute | solution.py:369
  505.1 5.3 kernel_M3.1
  510.4 5.3 kernel_M4.1
  515.7 5.3 %all-to-all-done.15.refs_0_ = bf16[4,8,48,384]{3,2,1,0:T(8,128)(2,1)S(1)} async-done(((bf16[4,8,48,384]{3,2,1,0:T(8,128)(2,1)}), bf16[4,8,48,384]{3,2,1,0:T(8,128)(2,1)S(1)}, u32[]{:S(2)}, u32[]{:S(2)}) %all-to-all-start.15) | async-done | bytes 1179680 | tf_op jit(solution)/shard_map/share_r5/all_to_all | solution.py:374
  522.0 5.2 kernel_M5.1
  (145 shorter events, 173.1 us)
Async XLA Ops:
  55.3 53.5 %collective-permute-start.6 = (bf16[12,192,384]{2,1,0:T(8,128)(2,1)S(1)}, bf16[12,192,384]{2,1,0:T(8,128)(2,1)}, u32[]{:S(2)}, u32[]{:S(2)}) collective-permute-start(bf16[12,192,384]{2,1,0:T(8,128)(2,1)S(1)} %copy-done.3), channel_id=1, source_target_pairs={{0,1},{1,0},{2,3},{3,2},{4,5},{5,4},{6,7},{7,6},{8,9},{9,8},{10,11... | collective-permute-start | bytes 5308424 | tf_op jit(solution)/shard_map/send_y0/ppermute | solution.py:369
  70.2 58.5 %collective-permute-start.8 = (bf16[4,8,48,384]{3,2,1,0:T(8,128)(2,1)}, bf16[4,8,48,384]{3,2,1,0:T(8,128)(2,1)}, u32[]{:S(2)}, u32[]{:S(2)}) collective-permute-start(bf16[4,8,48,384]{3,2,1,0:T(8,128)(2,1)} %all_to_all.90.refs_1_), channel_id=1, source_target_pairs={{8,16},{10,18},{12,20},{14,22},{16,8},{18,10},{20,12},{22,14},{9,1... | collective-permute-start | bytes 3538952 | tf_op jit(solution)/shard_map/send_a0/ppermute | solution.py:369
  72.0 58.4 %collective-permute-start.10 = (bf16[4,8,48,384]{3,2,1,0:T(8,128)(2,1)}, bf16[4,8,48,384]{3,2,1,0:T(8,128)(2,1)}, u32[]{:S(2)}, u32[]{:S(2)}) collective-permute-start(bf16[4,8,48,384]{3,2,1,0:T(8,128)(2,1)} %all-to-all-done.3.refs_5_), channel_id=1, source_target_pairs={{0,8},{2,10},{4,12},{6,14},{24,16},{26,18},{28,20},{30,22},{1,9},{... | collective-permute-start | bytes 3538952 | tf_op jit(solution)/shard_map/send_v0/ppermute | solution.py:369
  79.0 58.7 %collective-permute-start.11 = (bf16[4,8,48,384]{3,2,1,0:T(8,128)(2,1)}, bf16[4,8,48,384]{3,2,1,0:T(8,128)(2,1)}, u32[]{:S(2)}, u32[]{:S(2)}) collective-permute-start(bf16[4,8,48,384]{3,2,1,0:T(8,128)(2,1)} %all-to-all-done.4.refs_1_), channel_id=1, source_target_pairs={{0,8},{2,10},{4,12},{6,14},{24,16},{26,18},{28,20},{30,22},{1,9},{... | collective-permute-start | bytes 3538952 | tf_op jit(solution)/shard_map/send_n1/ppermute | solution.py:369
  81.4 58.7 %collective-permute-start.9 = (bf16[4,8,48,384]{3,2,1,0:T(8,128)(2,1)}, bf16[4,8,48,384]{3,2,1,0:T(8,128)(2,1)}, u32[]{:S(2)}, u32[]{:S(2)}) collective-permute-start(bf16[4,8,48,384]{3,2,1,0:T(8,128)(2,1)} %collective-permute-done.7.refs_2_), channel_id=1, source_target_pairs={{8,16},{10,18},{12,20},{14,22},{16,8},{18,10},{20,12},{22,14},{9,1... | collective-permute-start | bytes 3538952 | tf_op jit(solution)/shard_map/send_b0/ppermute | solution.py:369
  108.8 60.0 %collective-permute-start.5 = (bf16[12,192,384]{2,1,0:T(8,128)(2,1)S(1)}, bf16[12,192,384]{2,1,0:T(8,128)(2,1)}, u32[]{:S(2)}, u32[]{:S(2)}) collective-permute-start(bf16[12,192,384]{2,1,0:T(8,128)(2,1)S(1)} %copy-done.2), channel_id=1, source_target_pairs={{0,1},{1,0},{2,3},{3,2},{4,5},{5,4},{6,7},{7,6},{8,9},{9,8},{10,11... | collective-permute-start | bytes 5308424 | tf_op jit(solution)/shard_map/send_y1/ppermute | solution.py:369
  124.4 40.0 %all-to-all-start.1 = ((bf16[4,8,48,384]{3,2,1,0:T(8,128)(2,1)}), bf16[4,8,48,384]{3,2,1,0:T(8,128)(2,1)}, u32[]{:S(2)}, u32[]{:S(2)}) async-start(bf16[4,8,48,384]{3,2,1,0:T(8,128)(2,1)} %get-tuple-element.58), calls=%async_computation.1 | async-start | bytes 2359296 | tf_op jit(solution)/shard_map/share_u2/all_to_all | solution.py:374
  128.7 54.7 %collective-permute-start.12 = (bf16[4,8,48,384]{3,2,1,0:T(8,128)(2,1)}, bf16[4,8,48,384]{3,2,1,0:T(8,128)(2,1)}, u32[]{:S(2)}, u32[]{:S(2)}) collective-permute-start(bf16[4,8,48,384]{3,2,1,0:T(8,128)(2,1)} %all-to-all-done.4.refs_1_), channel_id=1, source_target_pairs={{8,16},{10,18},{12,20},{14,22},{16,8},{18,10},{20,12},{22,14},{9,1... | collective-permute-start | bytes 3538952 | tf_op jit(solution)/shard_map/send_a1/ppermute | solution.py:369
  130.4 54.7 %collective-permute-start.14 = (bf16[4,8,48,384]{3,2,1,0:T(8,128)(2,1)}, bf16[4,8,48,384]{3,2,1,0:T(8,128)(2,1)}, u32[]{:S(2)}, u32[]{:S(2)}) collective-permute-start(bf16[4,8,48,384]{3,2,1,0:T(8,128)(2,1)} %all-to-all-done.5.refs_5_), channel_id=1, source_target_pairs={{0,8},{2,10},{4,12},{6,14},{24,16},{26,18},{28,20},{30,22},{1,9},{... | collective-permute-start | bytes 3538952 | tf_op jit(solution)/shard_map/send_v1/ppermute | solution.py:369
  137.7 50.8 %collective-permute-start = (bf16[4,8,48,384]{3,2,1,0:T(8,128)(2,1)}, bf16[4,8,48,384]{3,2,1,0:T(8,128)(2,1)}, u32[]{:S(2)}, u32[]{:S(2)}) collective-permute-start(bf16[4,8,48,384]{3,2,1,0:T(8,128)(2,1)} %all-to-all-done.refs_1_), channel_id=1, source_target_pairs={{0,8},{2,10},{4,12},{6,14},{24,16},{26,18},{28,20},{30,22},{1,9},{... | collective-permute-start | bytes 3538952 | tf_op jit(solution)/shard_map/send_n2/ppermute | solution.py:369
  140.0 53.8 %collective-permute-start.13 = (bf16[4,8,48,384]{3,2,1,0:T(8,128)(2,1)}, bf16[4,8,48,384]{3,2,1,0:T(8,128)(2,1)}, u32[]{:S(2)}, u32[]{:S(2)}) collective-permute-start(bf16[4,8,48,384]{3,2,1,0:T(8,128)(2,1)} %collective-permute-done.11.refs_2_), channel_id=1, source_target_pairs={{8,16},{10,18},{12,20},{14,22},{16,8},{18,10},{20,12},{22,14},{9,1... | collective-permute-start | bytes 3538952 | tf_op jit(solution)/shard_map/send_b1/ppermute | solution.py:369
  168.8 54.4 %collective-permute-start.4 = (bf16[12,192,384]{2,1,0:T(8,128)(2,1)S(1)}, bf16[12,192,384]{2,1,0:T(8,128)(2,1)}, u32[]{:S(2)}, u32[]{:S(2)}) collective-permute-start(bf16[12,192,384]{2,1,0:T(8,128)(2,1)S(1)} %copy-done.1), channel_id=1, source_target_pairs={{0,1},{1,0},{2,3},{3,2},{4,5},{5,4},{6,7},{7,6},{8,9},{9,8},{10,11... | collective-permute-start | bytes 5308424 | tf_op jit(solution)/shard_map/send_y2/ppermute | solution.py:369
  183.4 58.2 %collective-permute-start.1 = (bf16[4,8,48,384]{3,2,1,0:T(8,128)(2,1)}, bf16[4,8,48,384]{3,2,1,0:T(8,128)(2,1)}, u32[]{:S(2)}, u32[]{:S(2)}) collective-permute-start(bf16[4,8,48,384]{3,2,1,0:T(8,128)(2,1)} %all-to-all-done.refs_1_), channel_id=1, source_target_pairs={{8,16},{10,18},{12,20},{14,22},{16,8},{18,10},{20,12},{22,14},{9,1... | collective-permute-start | bytes 3538952 | tf_op jit(solution)/shard_map/send_a2/ppermute | solution.py:369
  185.1 56.6 %collective-permute-start.3 = (bf16[4,8,48,384]{3,2,1,0:T(8,128)(2,1)}, bf16[4,8,48,384]{3,2,1,0:T(8,128)(2,1)}, u32[]{:S(2)}, u32[]{:S(2)}) collective-permute-start(bf16[4,8,48,384]{3,2,1,0:T(8,128)(2,1)} %all-to-all-done.1.refs_5_), channel_id=1, source_target_pairs={{0,8},{2,10},{4,12},{6,14},{24,16},{26,18},{28,20},{30,22},{1,9},{... | collective-permute-start | bytes 3538952 | tf_op jit(solution)/shard_map/send_v2/ppermute | solution.py:369
  188.5 53.2 %collective-permute-start.2 = (bf16[4,8,48,384]{3,2,1,0:T(8,128)(2,1)}, bf16[4,8,48,384]{3,2,1,0:T(8,128)(2,1)}, u32[]{:S(2)}, u32[]{:S(2)}) collective-permute-start(bf16[4,8,48,384]{3,2,1,0:T(8,128)(2,1)} %collective-permute-done.refs_2_), channel_id=1, source_target_pairs={{8,16},{10,18},{12,20},{14,22},{16,8},{18,10},{20,12},{22,14},{9,1... | collective-permute-start | bytes 3538952 | tf_op jit(solution)/shard_map/send_b2/ppermute | solution.py:369
  222.2 70.5 %collective-permute-start.22 = (bf16[12,192,384]{2,1,0:T(8,128)(2,1)S(1)}, bf16[12,192,384]{2,1,0:T(8,128)(2,1)}, u32[]{:S(2)}, u32[]{:S(2)}) collective-permute-start(bf16[12,192,384]{2,1,0:T(8,128)(2,1)S(1)} %copy-done), channel_id=1, source_target_pairs={{0,1},{1,0},{2,3},{3,2},{4,5},{5,4},{6,7},{7,6},{8,9},{9,8},{10,11... | collective-permute-start | bytes 5308424 | tf_op jit(solution)/shard_map/send_y3/ppermute | solution.py:369
  291.0 39.9 %collective-permute-start.24 = (bf16[4,8,48,384]{3,2,1,0:T(8,128)(2,1)}, bf16[4,8,48,384]{3,2,1,0:T(8,128)(2,1)}, u32[]{:S(2)}, u32[]{:S(2)}) collective-permute-start(bf16[4,8,48,384]{3,2,1,0:T(8,128)(2,1)} %all-to-all-done.11.refs_1_), channel_id=1, source_target_pairs={{8,16},{10,18},{12,20},{14,22},{16,8},{18,10},{20,12},{22,14},{9,1... | collective-permute-start | bytes 3538952 | tf_op jit(solution)/shard_map/send_a3/ppermute | solution.py:369
  292.7 39.9 %collective-permute-start.26 = (bf16[4,8,48,384]{3,2,1,0:T(8,128)(2,1)}, bf16[4,8,48,384]{3,2,1,0:T(8,128)(2,1)}, u32[]{:S(2)}, u32[]{:S(2)}) collective-permute-start(bf16[4,8,48,384]{3,2,1,0:T(8,128)(2,1)} %copy-done.18), channel_id=1, source_target_pairs={{0,8},{2,10},{4,12},{6,14},{24,16},{26,18},{28,20},{30,22},{1,9},{... | collective-permute-start | bytes 3538952 | tf_op jit(solution)/shard_map/send_v3/ppermute | solution.py:369
  302.0 53.0 %collective-permute-start.27 = (bf16[4,8,48,384]{3,2,1,0:T(8,128)(2,1)}, bf16[4,8,48,384]{3,2,1,0:T(8,128)(2,1)}, u32[]{:S(2)}, u32[]{:S(2)}) collective-permute-start(bf16[4,8,48,384]{3,2,1,0:T(8,128)(2,1)} %all-to-all-done.13.refs_1_), channel_id=1, source_target_pairs={{0,8},{2,10},{4,12},{6,14},{24,16},{26,18},{28,20},{30,22},{1,9},{... | collective-permute-start | bytes 3538952 | tf_op jit(solution)/shard_map/send_n4/ppermute | solution.py:369
  304.4 59.5 %collective-permute-start.25 = (bf16[4,8,48,384]{3,2,1,0:T(8,128)(2,1)}, bf16[4,8,48,384]{3,2,1,0:T(8,128)(2,1)}, u32[]{:S(2)}, u32[]{:S(2)}) collective-permute-start(bf16[4,8,48,384]{3,2,1,0:T(8,128)(2,1)} %collective-permute-done.23.refs_2_), channel_id=1, source_target_pairs={{8,16},{10,18},{12,20},{14,22},{16,8},{18,10},{20,12},{22,14},{9,1... | collective-permute-start | bytes 3538952 | tf_op jit(solution)/shard_map/send_b3/ppermute | solution.py:369
  308.5 51.9 %all-to-all-start.10 = ((bf16[4,8,48,384]{3,2,1,0:T(8,128)(2,1)}), bf16[4,8,48,384]{3,2,1,0:T(8,128)(2,1)S(1)}, u32[]{:S(2)}, u32[]{:S(2)}) async-start(bf16[4,8,48,384]{3,2,1,0:T(8,128)(2,1)} %broadcast_select_fusion.3), calls=%async_computation.10 | async-start | bytes 2359296 | tf_op jit(solution)/shard_map/share_r0/all_to_all | solution.py:374
  327.0 57.4 %collective-permute-start.19 = (bf16[4,8,48,384]{3,2,1,0:T(8,128)(2,1)}, bf16[4,8,48,384]{3,2,1,0:T(8,128)(2,1)}, u32[]{:S(2)}, u32[]{:S(2)}) collective-permute-start(bf16[4,8,48,384]{3,2,1,0:T(8,128)(2,1)} %get-tuple-element.75), channel_id=1, source_target_pairs={{8,0},{10,2},{12,4},{14,6},{16,24},{18,26},{20,28},{22,30},{9,1},{... | collective-permute-start | bytes 3538952 | tf_op jit(solution)/shard_map/send_o2/ppermute | solution.py:369
  330.9 62.5 %collective-permute-start.28 = (bf16[4,8,48,384]{3,2,1,0:T(8,128)(2,1)}, bf16[4,8,48,384]{3,2,1,0:T(8,128)(2,1)}, u32[]{:S(2)}, u32[]{:S(2)}) collective-permute-start(bf16[4,8,48,384]{3,2,1,0:T(8,128)(2,1)} %all-to-all-done.13.refs_1_), channel_id=1, source_target_pairs={{8,16},{10,18},{12,20},{14,22},{16,8},{18,10},{20,12},{22,14},{9,1... | collective-permute-start | bytes 3538952 | tf_op jit(solution)/shard_map/send_a4/ppermute | solution.py:369
  332.6 62.5 %collective-permute-start.30 = (bf16[4,8,48,384]{3,2,1,0:T(8,128)(2,1)S(1)}, bf16[4,8,48,384]{3,2,1,0:T(8,128)(2,1)}, u32[]{:S(2)}, u32[]{:S(2)}) collective-permute-start(bf16[4,8,48,384]{3,2,1,0:T(8,128)(2,1)S(1)} %copy-done.17), channel_id=1, source_target_pairs={{0,8},{2,10},{4,12},{6,14},{24,16},{26,18},{28,20},{30,22},{1,9},{... | collective-permute-start | bytes 3538952 | tf_op jit(solution)/shard_map/send_v4/ppermute | solution.py:369
  354.9 50.6 %collective-permute-start.15 = (bf16[4,8,48,384]{3,2,1,0:T(8,128)(2,1)}, bf16[4,8,48,384]{3,2,1,0:T(8,128)(2,1)}, u32[]{:S(2)}, u32[]{:S(2)}) collective-permute-start(bf16[4,8,48,384]{3,2,1,0:T(8,128)(2,1)} %all-to-all-done.6.refs_1_), channel_id=1, source_target_pairs={{0,8},{2,10},{4,12},{6,14},{24,16},{26,18},{28,20},{30,22},{1,9},{... | collective-permute-start | bytes 3538952 | tf_op jit(solution)/shard_map/send_n5/ppermute | solution.py:369
  360.4 40.7 %all-to-all-start.9 = ((bf16[4,8,48,384]{3,2,1,0:T(8,128)(2,1)}), bf16[4,8,48,384]{3,2,1,0:T(8,128)(2,1)S(1)}, u32[]{:S(2)}, u32[]{:S(2)}) async-start(bf16[4,8,48,384]{3,2,1,0:T(8,128)(2,1)} %broadcast_select_fusion.4), calls=%async_computation.9 | async-start | bytes 2359296 | tf_op jit(solution)/shard_map/share_r1/all_to_all | solution.py:374
  363.9 43.3 %collective-permute-start.29 = (bf16[4,8,48,384]{3,2,1,0:T(8,128)(2,1)}, bf16[4,8,48,384]{3,2,1,0:T(8,128)(2,1)}, u32[]{:S(2)}, u32[]{:S(2)}) collective-permute-start(bf16[4,8,48,384]{3,2,1,0:T(8,128)(2,1)} %collective-permute-done.27.refs_2_), channel_id=1, source_target_pairs={{8,16},{10,18},{12,20},{14,22},{16,8},{18,10},{20,12},{22,14},{9,1... | collective-permute-start | bytes 3538952 | tf_op jit(solution)/shard_map/send_b4/ppermute | solution.py:369
  384.4 54.3 %collective-permute-start.33 = (bf16[4,8,48,384]{3,2,1,0:T(8,128)(2,1)}, bf16[4,8,48,384]{3,2,1,0:T(8,128)(2,1)}, u32[]{:S(2)}, u32[]{:S(2)}) collective-permute-start(bf16[4,8,48,384]{3,2,1,0:T(8,128)(2,1)} %get-tuple-element.97), channel_id=1, source_target_pairs={{8,0},{10,2},{12,4},{14,6},{16,24},{18,26},{20,28},{22,30},{9,1},{... | collective-permute-start | bytes 3538952 | tf_op jit(solution)/shard_map/send_o3/ppermute | solution.py:369
  393.4 51.5 %collective-permute-start.16 = (bf16[4,8,48,384]{3,2,1,0:T(8,128)(2,1)}, bf16[4,8,48,384]{3,2,1,0:T(8,128)(2,1)}, u32[]{:S(2)}, u32[]{:S(2)}) collective-permute-start(bf16[4,8,48,384]{3,2,1,0:T(8,128)(2,1)} %all-to-all-done.6.refs_1_), channel_id=1, source_target_pairs={{8,16},{10,18},{12,20},{14,22},{16,8},{18,10},{20,12},{22,14},{9,1... | collective-permute-start | bytes 3538952 | tf_op jit(solution)/shard_map/send_a5/ppermute | solution.py:369
  395.1 49.8 %collective-permute-start.18 = (bf16[4,8,48,384]{3,2,1,0:T(8,128)(2,1)}, bf16[4,8,48,384]{3,2,1,0:T(8,128)(2,1)}, u32[]{:S(2)}, u32[]{:S(2)}) collective-permute-start(bf16[4,8,48,384]{3,2,1,0:T(8,128)(2,1)} %all-to-all-done.7.refs_5_), channel_id=1, source_target_pairs={{0,8},{2,10},{4,12},{6,14},{24,16},{26,18},{28,20},{30,22},{1,9},{... | collective-permute-start | bytes 3538952 | tf_op jit(solution)/shard_map/send_v5/ppermute | solution.py:369
  405.5 39.4 %collective-permute-start.17 = (bf16[4,8,48,384]{3,2,1,0:T(8,128)(2,1)}, bf16[4,8,48,384]{3,2,1,0:T(8,128)(2,1)}, u32[]{:S(2)}, u32[]{:S(2)}) collective-permute-start(bf16[4,8,48,384]{3,2,1,0:T(8,128)(2,1)} %collective-permute-done.15.refs_2_), channel_id=1, source_target_pairs={{8,16},{10,18},{12,20},{14,22},{16,8},{18,10},{20,12},{22,14},{9,1... | collective-permute-start | bytes 3538952 | tf_op jit(solution)/shard_map/send_b5/ppermute | solution.py:369
  425.7 39.1 %collective-permute-start.32 = (bf16[4,8,48,384]{3,2,1,0:T(8,128)(2,1)}, bf16[4,8,48,384]{3,2,1,0:T(8,128)(2,1)S(1)}, u32[]{:S(2)}, u32[]{:S(2)}) collective-permute-start(bf16[4,8,48,384]{3,2,1,0:T(8,128)(2,1)} %get-tuple-element.96), channel_id=1, source_target_pairs={{8,0},{10,2},{12,4},{14,6},{16,24},{18,26},{20,28},{22,30},{9,1},{... | collective-permute-start | bytes 3538952 | tf_op jit(solution)/shard_map/send_o4/ppermute | solution.py:369
  (39 other events, 723.5 us)

commit v3 on v2

--- a/solution.py
+++ b/solution.py
@@ -185,24 +185,18 @@
         columns.append(jnp.concatenate(blocks, axis=0) if n_in > 1 else blocks[0])
     field = decode_scalar(jnp.concatenate(columns, axis=1))
     high, low = split(field)
-    start = 0
+    deep = table_ref.shape[3]
+    both = dot(table_ref[...].reshape(-1, deep), high)
+    tall = both.shape[0] // 2
+    spread = both[:tall] + both[tall:] + dot(table_ref[0].reshape(tall, deep), low)
+    half = tall // (2 * n_out)
     for o in range(n_out):
-        parts, nx = u_refs[o].shape[0], u_refs[o].shape[2]
-        bunch = 4
-        for s in range(0, parts, bunch):
-            tall = bunch * nx
-            pair = []
-            for which in range(2):
-                t_high = table_ref[0, which, pl.ds(start, tall), :]
-                t_low = table_ref[1, which, pl.ds(start, tall), :]
-                pair.append(dot3(t_high, t_low, high, low))
-            for k in range(rows):
-                cols = slice(k * nz, (k + 1) * nz)
-                u = u_refs[o][s:s + bunch, k].astype(F32).reshape(tall, nz)
-                value = u * pair[0][:, cols] + pair[1][:, cols]
-                coded = encode_stream(value, rate).astype(BF16)
-                s_refs[o][s:s + bunch, k] = coded.reshape(bunch, nx, nz)
-            start += tall
+        first, second = spread[o * half:(o + 1) * half], spread[tall // 2 + o * half:tall // 2 + (o + 1) * half]
+        for k in range(rows):
+            cols = slice(k * nz, (k + 1) * nz)
+            u = u_refs[o][:, k].astype(F32).reshape(half, nz)
+            value = u * first[:, cols] + second[:, cols]
+            s_refs[o][:, k] = encode_stream(value, rate).astype(BF16).reshape(s_refs[o].shape[0], -1, nz)
 
 
 def stream(table, fields, speeds, rate, after):
@@ -241,7 +235,8 @@
         )
 
     y_high, y_low = stack(own_high, other_high), stack(own_low, other_low)
-    slope = dot3(wall_ref[0], wall_ref[1], y_high, y_low)
+    both = dot(wall_ref[...].reshape(2 * ny, -1), y_high)
+    slope = both[:ny] + both[ny:] + dot(wall_ref[0], y_low)
     z_high, z_low = own_high.reshape(-1, nz), own_low.reshape(-1, nz)
     span = dot3(z_high, z_low, span_ref[0], span_ref[1])
     for x in range(planes):

time: 536 us -> 532 us (level)
  Pallas kernels: 240 us -> 231 us
    pallas_call x26, Pallas kernels: 240 us -> 231 us  [launch(): pl.pallas_call(run, in_specs=list(in_specs) + [pl.BlockSpec(memory_space=...]
  transfers between devices with their start and end apart: 51 -> 51, of which waited for: 11 -> 11; matrix products, arithmetic and copies ran while one was open for 3% -> 3% of each run, Pallas kernels for 44% -> 42%
where the time goes in v3:
time: 532 us; the launch traced here: 524 us
  Pallas kernels  231 us (43%)
  starting transfers between devices  166 us (31%)
  waiting for transfers between devices  82.9 us (16%)
  blocking collectives  20.8 us (4%)
  other arithmetic  13.3 us (2%)
  local copies, waits for them, and re-layouts  8.31 us (2%)
    pallas_call x26, Pallas kernels, launch(): pl.pallas_call(run, in_specs=list(in_specs) + [pl.BlockSpec(memory_space=...  231 us
    ppermute x34, starting transfers between devices, send(): made[name] = lax.ppermute(x, axis, pairs)  97.3 us
    all_to_all x17, starting transfers between devices, share(): lax.all_to_all(x, 'px', 0, 0, axis_index_groups=groups, tiled=True)  68.4 us
    ppermute x34, waiting for transfers between devices, send(): made[name] = lax.ppermute(x, axis, pairs)  52.9 us
    all_to_all x17, waiting for transfers between devices, share(): lax.all_to_all(x, 'px', 0, 0, axis_index_groups=groups, tiled=True)  30 us
    all_to_all x1, blocking collectives, share(): lax.all_to_all(x, 'px', 0, 0, axis_index_groups=groups, tiled=True)  20.8 us
    select_n x6, other arithmetic, body(): made[f's{c}'] = s = jnp.where(outer, got, s_own)  13.3 us
  transfers between devices with their start and end apart: 51, of which 11 were waited for; matrix products, arithmetic and copies ran while one was open for 3% of the time, Pallas kernels for 42%

profile of v3, /device:TPU:0, one launch (start us, length us, event | category | flops | bytes accessed | tf_op | source)
XLA Modules:
  0.0 523.5 jit_solution(14243015973748299517)
XLA Ops:
  4.5 20.8 %all_to_all.90.refs_1_ = bf16[4,8,48,384]{3,2,1,0:T(8,128)(2,1)} all-to-all(bf16[4,8,48,384]{3,2,1,0:T(8,128)(2,1)} %get-tuple-element.55.refs_1_), channel_id=1, replica_groups={{0,2,4,6},{8,10,12,14},{16,18,20,22},{24,26,28,30},{1,3,5,7},{9,11,13,1..., dimensions={0} | all-to-all | bytes 2359296 | tf_op jit(solution)/shard_map/share_g0/all_to_all | solution.py:369
  37.9 7.7 %all-to-all-done.3.refs_5_ = bf16[4,8,48,384]{3,2,1,0:T(8,128)(2,1)} async-done(((bf16[4,8,48,384]{3,2,1,0:T(8,128)(2,1)}), bf16[4,8,48,384]{3,2,1,0:T(8,128)(2,1)}, u32[]{:S(2)}, u32[]{:S(2)}) %all-to-all-start.3) | async-done | bytes 1179680 | tf_op jit(solution)/shard_map/share_u0/all_to_all | solution.py:369
  50.0 5.3 %collective-permute-start.7 = (bf16[4,8,48,384]{3,2,1,0:T(8,128)(2,1)}, bf16[4,8,48,384]{3,2,1,0:T(8,128)(2,1)}, u32[]{:S(2)}, u32[]{:S(2)}) collective-permute-start(bf16[4,8,48,384]{3,2,1,0:T(8,128)(2,1)} %all_to_all.90.refs_1_), channel_id=1, source_target_pairs={{0,8},{2,10},{4,12},{6,14},{24,16},{26,18},{28,20},{30,22},{1,9},{... | collective-permute-start | bytes 3538952 | tf_op jit(solution)/shard_map/send_n0/ppermute | solution.py:364
  56.8 9.1 %all-to-all-done.4.refs_1_ = bf16[4,8,48,384]{3,2,1,0:T(8,128)(2,1)} async-done(((bf16[4,8,48,384]{3,2,1,0:T(8,128)(2,1)}), bf16[4,8,48,384]{3,2,1,0:T(8,128)(2,1)}, u32[]{:S(2)}, u32[]{:S(2)}) %all-to-all-start.4) | async-done | bytes 1179680 | tf_op jit(solution)/shard_map/share_g1/all_to_all | solution.py:369
  72.0 7.1 %collective-permute-start.10 = (bf16[4,8,48,384]{3,2,1,0:T(8,128)(2,1)}, bf16[4,8,48,384]{3,2,1,0:T(8,128)(2,1)}, u32[]{:S(2)}, u32[]{:S(2)}) collective-permute-start(bf16[4,8,48,384]{3,2,1,0:T(8,128)(2,1)} %all-to-all-done.3.refs_5_), channel_id=1, source_target_pairs={{0,8},{2,10},{4,12},{6,14},{24,16},{26,18},{28,20},{30,22},{1,9},{... | collective-permute-start | bytes 3538952 | tf_op jit(solution)/shard_map/send_v0/ppermute | solution.py:364
  110.3 13.9 %kernel_L0.1 = (f32[48,192,384]{2,1,0:T(8,128)}, f32[48,192,384]{2,1,0:T(8,128)}, f32[8,128]{1,0:T(8,128)}) custom-call(bf16[2,192,384]{2,1,0:T(8,128)(2,1)} %dynamic-slice_bitcast_fusion.1.refs_0_, bf16[2,384,768]{2,1,0:T(8,128)(2,1)} %constant.49.clone.refs_1_, f32[48,192,384]{2,1,0:T(8,128)} %refs_2_.7, ...), custom_call_target="tpu_custom_call" | custom-call | flops 6115295232 | bytes 19464192 | tf_op jit(solution)/shard_map/kernel_L0/pallas_call | solution.py:119
  130.2 7.3 %collective-permute-start.14 = (bf16[4,8,48,384]{3,2,1,0:T(8,128)(2,1)}, bf16[4,8,48,384]{3,2,1,0:T(8,128)(2,1)}, u32[]{:S(2)}, u32[]{:S(2)}) collective-permute-start(bf16[4,8,48,384]{3,2,1,0:T(8,128)(2,1)} %all-to-all-done.5.refs_5_), channel_id=1, source_target_pairs={{0,8},{2,10},{4,12},{6,14},{24,16},{26,18},{28,20},{30,22},{1,9},{... | collective-permute-start | bytes 3538952 | tf_op jit(solution)/shard_map/send_v1/ppermute | solution.py:364
  141.8 17.1 %kernel_X0.1 = (bf16[4,8,48,384]{3,2,1,0:T(8,128)(2,1)}, bf16[4,8,48,384]{3,2,1,0:T(8,128)(2,1)}) custom-call(bf16[2,2,384,768]{3,2,1,0:T(8,128)(2,1)} %dynamic-slice_bitcast_fusion.refs_0_, bf16[4,8,48,384]{3,2,1,0:T(8,128)(2,1)} %all_to_all.90.refs_1_, bf16[4,8,48,384]{3,2,1,0:T(8,128)(2,1)} %collective-permute-done.7.refs_2_, ...), custom_call_target="tpu_custom_call" | custom-call | flops 10871635968 | bytes 9437184 | tf_op jit(solution)/shard_map/kernel_X0/pallas_call | solution.py:119
  167.9 13.8 %kernel_L1.1 = (f32[48,192,384]{2,1,0:T(8,128)}, f32[48,192,384]{2,1,0:T(8,128)}, f32[8,128]{1,0:T(8,128)}) custom-call(bf16[2,192,384]{2,1,0:T(8,128)(2,1)} %dynamic-slice_bitcast_fusion.1.refs_0_, bf16[2,384,768]{2,1,0:T(8,128)(2,1)} %constant.49.clone.refs_1_, f32[48,192,384]{2,1,0:T(8,128)} %refs_2_.7, ...), custom_call_target="tpu_custom_call", output_to_operand_aliasing={{0}: (7, {}), {1}: (8, {})} | custom-call | flops 6115295232 | bytes 19464192 | tf_op jit(solution)/shard_map/kernel_L1/pallas_call | solution.py:119
  193.7 17.2 %kernel_X1.1 = (bf16[4,8,48,384]{3,2,1,0:T(8,128)(2,1)}, bf16[4,8,48,384]{3,2,1,0:T(8,128)(2,1)}) custom-call(bf16[2,2,384,768]{3,2,1,0:T(8,128)(2,1)} %dynamic-slice_bitcast_fusion.refs_0_, bf16[4,8,48,384]{3,2,1,0:T(8,128)(2,1)} %all-to-all-done.4.refs_1_, bf16[4,8,48,384]{3,2,1,0:T(8,128)(2,1)} %collective-permute-done.11.refs_2_, ...), custom_call_target="tpu_custom_call" | custom-call | flops 10871635968 | bytes 9437184 | tf_op jit(solution)/shard_map/kernel_X1/pallas_call | solution.py:119
  215.9 4.9 all-to-all-start.13
  221.4 13.8 %kernel_L2.1 = (f32[48,192,384]{2,1,0:T(8,128)}, f32[48,192,384]{2,1,0:T(8,128)}, f32[8,128]{1,0:T(8,128)}) custom-call(bf16[2,192,384]{2,1,0:T(8,128)(2,1)} %dynamic-slice_bitcast_fusion.1.refs_0_, bf16[2,384,768]{2,1,0:T(8,128)(2,1)} %constant.49.clone.refs_1_, f32[48,192,384]{2,1,0:T(8,128)} %refs_2_.7, ...), custom_call_target="tpu_custom_call", output_to_operand_aliasing={{0}: (7, {}), {1}: (8, {})} | custom-call | flops 6115295232 | bytes 19464192 | tf_op jit(solution)/shard_map/kernel_L2/pallas_call | solution.py:119
  240.3 17.2 %kernel_X2.1 = (bf16[4,8,48,384]{3,2,1,0:T(8,128)(2,1)}, bf16[4,8,48,384]{3,2,1,0:T(8,128)(2,1)}) custom-call(bf16[2,2,384,768]{3,2,1,0:T(8,128)(2,1)} %dynamic-slice_bitcast_fusion.refs_0_, bf16[4,8,48,384]{3,2,1,0:T(8,128)(2,1)} %all-to-all-done.refs_1_, bf16[4,8,48,384]{3,2,1,0:T(8,128)(2,1)} %collective-permute-done.refs_2_, ...), custom_call_target="tpu_custom_call" | custom-call | flops 10871635968 | bytes 9437184 | tf_op jit(solution)/shard_map/kernel_X2/pallas_call | solution.py:119
  268.0 8.2 %collective-permute-start.23 = (bf16[4,8,48,384]{3,2,1,0:T(8,128)(2,1)}, bf16[4,8,48,384]{3,2,1,0:T(8,128)(2,1)}, u32[]{:S(2)}, u32[]{:S(2)}) collective-permute-start(bf16[4,8,48,384]{3,2,1,0:T(8,128)(2,1)} %all-to-all-done.11.refs_1_), channel_id=1, source_target_pairs={{0,8},{2,10},{4,12},{6,14},{24,16},{26,18},{28,20},{30,22},{1,9},{... | collective-permute-start | bytes 3538952 | tf_op jit(solution)/shard_map/send_n3/ppermute | solution.py:364
  276.2 6.4 %all-to-all-done.6.refs_1_ = bf16[4,8,48,384]{3,2,1,0:T(8,128)(2,1)} async-done(((bf16[4,8,48,384]{3,2,1,0:T(8,128)(2,1)}), bf16[4,8,48,384]{3,2,1,0:T(8,128)(2,1)}, u32[]{:S(2)}, u32[]{:S(2)}) %all-to-all-start.6) | async-done | bytes 1179680 | tf_op jit(solution)/shard_map/share_g5/all_to_all | solution.py:369
  290.1 8.9 %collective-permute-start.26 = (bf16[4,8,48,384]{3,2,1,0:T(8,128)(2,1)}, bf16[4,8,48,384]{3,2,1,0:T(8,128)(2,1)}, u32[]{:S(2)}, u32[]{:S(2)}) collective-permute-start(bf16[4,8,48,384]{3,2,1,0:T(8,128)(2,1)} %copy-done.18), channel_id=1, source_target_pairs={{0,8},{2,10},{4,12},{6,14},{24,16},{26,18},{28,20},{30,22},{1,9},{... | collective-permute-start | bytes 3538952 | tf_op jit(solution)/shard_map/send_v3/ppermute | solution.py:364
  309.4 13.9 %kernel_L3.1 = (f32[48,192,384]{2,1,0:T(8,128)}, f32[48,192,384]{2,1,0:T(8,128)}, f32[8,128]{1,0:T(8,128)}) custom-call(bf16[2,192,384]{2,1,0:T(8,128)(2,1)} %dynamic-slice_bitcast_fusion.1.refs_0_, bf16[2,384,768]{2,1,0:T(8,128)(2,1)} %constant.49.clone.refs_1_, f32[48,192,384]{2,1,0:T(8,128)} %refs_2_.7, ...), custom_call_target="tpu_custom_call", output_to_operand_aliasing={{0}: (7, {}), {1}: (8, {})} | custom-call | flops 6115295232 | bytes 19464192 | tf_op jit(solution)/shard_map/kernel_L3/pallas_call | solution.py:119
  329.9 6.0 %collective-permute-start.30 = (bf16[4,8,48,384]{3,2,1,0:T(8,128)(2,1)S(1)}, bf16[4,8,48,384]{3,2,1,0:T(8,128)(2,1)}, u32[]{:S(2)}, u32[]{:S(2)}) collective-permute-start(bf16[4,8,48,384]{3,2,1,0:T(8,128)(2,1)S(1)} %copy-done.17), channel_id=1, source_target_pairs={{0,8},{2,10},{4,12},{6,14},{24,16},{26,18},{28,20},{30,22},{1,9},{... | collective-permute-start | bytes 3538952 | tf_op jit(solution)/shard_map/send_v4/ppermute | solution.py:364
  336.0 16.3 %collective-permute-done.27.refs_2_ = bf16[4,8,48,384]{3,2,1,0:T(8,128)(2,1)} collective-permute-done((bf16[4,8,48,384]{3,2,1,0:T(8,128)(2,1)}, bf16[4,8,48,384]{3,2,1,0:T(8,128)(2,1)}, u32[]{:S(2)}, u32[]{:S(2)}) %collective-permute-start.27) | collective-permute-done | bytes 1179680 | tf_op jit(solution)/shard_map/send_n4/ppermute | solution.py:364
  352.3 5.4 %collective-permute-start.15 = (bf16[4,8,48,384]{3,2,1,0:T(8,128)(2,1)}, bf16[4,8,48,384]{3,2,1,0:T(8,128)(2,1)}, u32[]{:S(2)}, u32[]{:S(2)}) collective-permute-start(bf16[4,8,48,384]{3,2,1,0:T(8,128)(2,1)} %all-to-all-done.6.refs_1_), channel_id=1, source_target_pairs={{0,8},{2,10},{4,12},{6,14},{24,16},{26,18},{28,20},{30,22},{1,9},{... | collective-permute-start | bytes 3538952 | tf_op jit(solution)/shard_map/send_n5/ppermute | solution.py:364
  363.2 17.2 %kernel_X3.1 = (bf16[4,8,48,384]{3,2,1,0:T(8,128)(2,1)}, bf16[4,8,48,384]{3,2,1,0:T(8,128)(2,1)}) custom-call(bf16[2,2,384,768]{3,2,1,0:T(8,128)(2,1)} %dynamic-slice_bitcast_fusion.refs_0_, bf16[4,8,48,384]{3,2,1,0:T(8,128)(2,1)} %all-to-all-done.11.refs_1_, bf16[4,8,48,384]{3,2,1,0:T(8,128)(2,1)} %collective-permute-done.23.refs_2_, ...), custom_call_target="tpu_custom_call" | custom-call | flops 10871635968 | bytes 9437184 | tf_op jit(solution)/shard_map/kernel_X3/pallas_call | solution.py:119
  384.2 5.2 %kernel_M0.1 = (f32[48,192,384]{2,1,0:T(8,128)}, f32[48,192,384]{2,1,0:T(8,128)}, f32[8,128]{1,0:T(8,128)}) custom-call(bf16[4,8,48,384]{3,2,1,0:T(8,128)(2,1)} %copy-done.11, f32[48,192,384]{2,1,0:T(8,128)} %get-tuple-element.80.refs_1_, f32[48,192,384]{2,1,0:T(8,128)} %get-tuple-element.81.refs_2_, ...), custom_call_target="tpu_custom_call", output_to_operand_aliasing={{0}: (1, {}), {1}: (2, {})} | custom-call | bytes 10616832 | tf_op jit(solution)/shard_map/kernel_M0/pallas_call | solution.py:119
  391.2 5.9 %collective-permute-start.18 = (bf16[4,8,48,384]{3,2,1,0:T(8,128)(2,1)}, bf16[4,8,48,384]{3,2,1,0:T(8,128)(2,1)}, u32[]{:S(2)}, u32[]{:S(2)}) collective-permute-start(bf16[4,8,48,384]{3,2,1,0:T(8,128)(2,1)} %all-to-all-done.7.refs_5_), channel_id=1, source_target_pairs={{0,8},{2,10},{4,12},{6,14},{24,16},{26,18},{28,20},{30,22},{1,9},{... | collective-permute-start | bytes 3538952 | tf_op jit(solution)/shard_map/send_v5/ppermute | solution.py:364
  404.6 17.2 %kernel_X4.1 = (bf16[4,8,48,384]{3,2,1,0:T(8,128)(2,1)}, bf16[4,8,48,384]{3,2,1,0:T(8,128)(2,1)}) custom-call(bf16[2,2,384,768]{3,2,1,0:T(8,128)(2,1)} %dynamic-slice_bitcast_fusion.refs_0_, bf16[4,8,48,384]{3,2,1,0:T(8,128)(2,1)} %all-to-all-done.13.refs_1_, bf16[4,8,48,384]{3,2,1,0:T(8,128)(2,1)} %collective-permute-done.27.refs_2_, ...), custom_call_target="tpu_custom_call" | custom-call | flops 10871635968 | bytes 9437184 | tf_op jit(solution)/shard_map/kernel_X4/pallas_call | solution.py:119
  423.0 5.3 %kernel_M1.1 = (f32[48,192,384]{2,1,0:T(8,128)}, f32[48,192,384]{2,1,0:T(8,128)}, f32[8,128]{1,0:T(8,128)}) custom-call(bf16[4,8,48,384]{3,2,1,0:T(8,128)(2,1)} %copy-done.10, f32[48,192,384]{2,1,0:T(8,128)} %get-tuple-element.85.refs_1_, f32[48,192,384]{2,1,0:T(8,128)} %get-tuple-element.86.refs_2_, ...), custom_call_target="tpu_custom_call", output_to_operand_aliasing={{0}: (1, {}), {1}: (2, {})} | custom-call | bytes 10616832 | tf_op jit(solution)/shard_map/kernel_M1/pallas_call | solution.py:119
  429.4 5.3 %kernel_M2.1 = (f32[48,192,384]{2,1,0:T(8,128)}, f32[48,192,384]{2,1,0:T(8,128)}, f32[8,128]{1,0:T(8,128)}) custom-call(bf16[4,8,48,384]{3,2,1,0:T(8,128)(2,1)} %copy-done.4, f32[48,192,384]{2,1,0:T(8,128)} %get-tuple-element.90.refs_1_, f32[48,192,384]{2,1,0:T(8,128)} %get-tuple-element.91.refs_2_, ...), custom_call_target="tpu_custom_call", output_to_operand_aliasing={{0}: (1, {}), {1}: (2, {})} | custom-call | bytes 10616832 | tf_op jit(solution)/shard_map/kernel_M2/pallas_call | solution.py:119
  441.0 17.2 %kernel_X5.1 = (bf16[4,8,48,384]{3,2,1,0:T(8,128)(2,1)}, bf16[4,8,48,384]{3,2,1,0:T(8,128)(2,1)}) custom-call(bf16[2,2,384,768]{3,2,1,0:T(8,128)(2,1)} %dynamic-slice_bitcast_fusion.refs_0_, bf16[4,8,48,384]{3,2,1,0:T(8,128)(2,1)} %all-to-all-done.6.refs_1_, bf16[4,8,48,384]{3,2,1,0:T(8,128)(2,1)} %collective-permute-done.15.refs_2_, ...), custom_call_target="tpu_custom_call" | custom-call | flops 10871635968 | bytes 9437184 | tf_op jit(solution)/shard_map/kernel_X5/pallas_call | solution.py:119
  464.5 30.7 %collective-permute-done.31 = bf16[4,8,48,384]{3,2,1,0:T(8,128)(2,1)} collective-permute-done((bf16[4,8,48,384]{3,2,1,0:T(8,128)(2,1)}, bf16[4,8,48,384]{3,2,1,0:T(8,128)(2,1)}, u32[]{:S(2)}, u32[]{:S(2)}) %collective-permute-start.31) | collective-permute-done | bytes 1179680 | tf_op jit(solution)/shard_map/send_o5/ppermute | solution.py:364
  501.2 5.3 %kernel_M3.1 = (f32[48,192,384]{2,1,0:T(8,128)}, f32[48,192,384]{2,1,0:T(8,128)}, f32[8,128]{1,0:T(8,128)}) custom-call(bf16[4,8,48,384]{3,2,1,0:T(8,128)(2,1)} %copy-done.12, f32[48,192,384]{2,1,0:T(8,128)} %get-tuple-element.98.refs_1_, f32[48,192,384]{2,1,0:T(8,128)} %get-tuple-element.99.refs_2_, ...), custom_call_target="tpu_custom_call", output_to_operand_aliasing={{0}: (1, {}), {1}: (2, {})} | custom-call | bytes 10616832 | tf_op jit(solution)/shard_map/kernel_M3/pallas_call | solution.py:119
  506.5 5.3 %kernel_M4.1 = (f32[48,192,384]{2,1,0:T(8,128)}, f32[48,192,384]{2,1,0:T(8,128)}, f32[8,128]{1,0:T(8,128)}) custom-call(bf16[4,8,48,384]{3,2,1,0:T(8,128)(2,1)} %copy-done.5, f32[48,192,384]{2,1,0:T(8,128)} %get-tuple-element.100.refs_1_, f32[48,192,384]{2,1,0:T(8,128)} %get-tuple-element.101.refs_2_, ...), custom_call_target="tpu_custom_call", output_to_operand_aliasing={{0}: (1, {}), {1}: (2, {})} | custom-call | bytes 10616832 | tf_op jit(solution)/shard_map/kernel_M4/pallas_call | solution.py:119
  511.7 5.3 %all-to-all-done.15.refs_0_ = bf16[4,8,48,384]{3,2,1,0:T(8,128)(2,1)S(1)} async-done(((bf16[4,8,48,384]{3,2,1,0:T(8,128)(2,1)}), bf16[4,8,48,384]{3,2,1,0:T(8,128)(2,1)S(1)}, u32[]{:S(2)}, u32[]{:S(2)}) %all-to-all-start.15) | async-done | bytes 1179680 | tf_op jit(solution)/shard_map/share_r5/all_to_all | solution.py:369
  518.0 5.2 %kernel_M5.1 = (f32[48,192,384]{2,1,0:T(8,128)}, f32[48,192,384]{2,1,0:T(8,128)}, f32[8,128]{1,0:T(8,128)}) custom-call(bf16[4,8,48,384]{3,2,1,0:T(8,128)(2,1)} %copy-done.6, f32[48,192,384]{2,1,0:T(8,128)} %get-tuple-element.103.refs_1_, f32[48,192,384]{2,1,0:T(8,128)} %get-tuple-element.104.refs_2_, ...), custom_call_target="tpu_custom_call", output_to_operand_aliasing={{0}: (1, {}), {1}: (2, {})} | custom-call | bytes 10616832 | tf_op jit(solution)/shard_map/kernel_M5/pallas_call | solution.py:119
  (145 shorter events, 176.5 us)
Async XLA Ops:
  55.3 53.5 %collective-permute-start.6 = (bf16[12,192,384]{2,1,0:T(8,128)(2,1)S(1)}, bf16[12,192,384]{2,1,0:T(8,128)(2,1)}, u32[]{:S(2)}, u32[]{:S(2)}) collective-permute-start(bf16[12,192,384]{2,1,0:T(8,128)(2,1)S(1)} %copy-done.3), channel_id=1, source_target_pairs={{0,1},{1,0},{2,3},{3,2},{4,5},{5,4},{6,7},{7,6},{8,9},{9,8},{10,11... | collective-permute-start | bytes 5308424 | tf_op jit(solution)/shard_map/send_y0/ppermute | solution.py:364
  70.2 58.3 %collective-permute-start.8 = (bf16[4,8,48,384]{3,2,1,0:T(8,128)(2,1)}, bf16[4,8,48,384]{3,2,1,0:T(8,128)(2,1)}, u32[]{:S(2)}, u32[]{:S(2)}) collective-permute-start(bf16[4,8,48,384]{3,2,1,0:T(8,128)(2,1)} %all_to_all.90.refs_1_), channel_id=1, source_target_pairs={{8,16},{10,18},{12,20},{14,22},{16,8},{18,10},{20,12},{22,14},{9,1... | collective-permute-start | bytes 3538952 | tf_op jit(solution)/shard_map/send_a0/ppermute | solution.py:364
  72.0 58.2 %collective-permute-start.10 = (bf16[4,8,48,384]{3,2,1,0:T(8,128)(2,1)}, bf16[4,8,48,384]{3,2,1,0:T(8,128)(2,1)}, u32[]{:S(2)}, u32[]{:S(2)}) collective-permute-start(bf16[4,8,48,384]{3,2,1,0:T(8,128)(2,1)} %all-to-all-done.3.refs_5_), channel_id=1, source_target_pairs={{0,8},{2,10},{4,12},{6,14},{24,16},{26,18},{28,20},{30,22},{1,9},{... | collective-permute-start | bytes 3538952 | tf_op jit(solution)/shard_map/send_v0/ppermute | solution.py:364
  79.0 58.5 %collective-permute-start.11 = (bf16[4,8,48,384]{3,2,1,0:T(8,128)(2,1)}, bf16[4,8,48,384]{3,2,1,0:T(8,128)(2,1)}, u32[]{:S(2)}, u32[]{:S(2)}) collective-permute-start(bf16[4,8,48,384]{3,2,1,0:T(8,128)(2,1)} %all-to-all-done.4.refs_1_), channel_id=1, source_target_pairs={{0,8},{2,10},{4,12},{6,14},{24,16},{26,18},{28,20},{30,22},{1,9},{... | collective-permute-start | bytes 3538952 | tf_op jit(solution)/shard_map/send_n1/ppermute | solution.py:364
  81.4 58.5 %collective-permute-start.9 = (bf16[4,8,48,384]{3,2,1,0:T(8,128)(2,1)}, bf16[4,8,48,384]{3,2,1,0:T(8,128)(2,1)}, u32[]{:S(2)}, u32[]{:S(2)}) collective-permute-start(bf16[4,8,48,384]{3,2,1,0:T(8,128)(2,1)} %collective-permute-done.7.refs_2_), channel_id=1, source_target_pairs={{8,16},{10,18},{12,20},{14,22},{16,8},{18,10},{20,12},{22,14},{9,1... | collective-permute-start | bytes 3538952 | tf_op jit(solution)/shard_map/send_b0/ppermute | solution.py:364
  108.8 58.5 %collective-permute-start.5 = (bf16[12,192,384]{2,1,0:T(8,128)(2,1)S(1)}, bf16[12,192,384]{2,1,0:T(8,128)(2,1)}, u32[]{:S(2)}, u32[]{:S(2)}) collective-permute-start(bf16[12,192,384]{2,1,0:T(8,128)(2,1)S(1)} %copy-done.2), channel_id=1, source_target_pairs={{0,1},{1,0},{2,3},{3,2},{4,5},{5,4},{6,7},{7,6},{8,9},{9,8},{10,11... | collective-permute-start | bytes 5308424 | tf_op jit(solution)/shard_map/send_y1/ppermute | solution.py:364
  124.2 38.7 %all-to-all-start.1 = ((bf16[4,8,48,384]{3,2,1,0:T(8,128)(2,1)}), bf16[4,8,48,384]{3,2,1,0:T(8,128)(2,1)}, u32[]{:S(2)}, u32[]{:S(2)}) async-start(bf16[4,8,48,384]{3,2,1,0:T(8,128)(2,1)} %get-tuple-element.58), calls=%async_computation.1 | async-start | bytes 2359296 | tf_op jit(solution)/shard_map/share_u2/all_to_all | solution.py:369
  128.5 53.2 %collective-permute-start.12 = (bf16[4,8,48,384]{3,2,1,0:T(8,128)(2,1)}, bf16[4,8,48,384]{3,2,1,0:T(8,128)(2,1)}, u32[]{:S(2)}, u32[]{:S(2)}) collective-permute-start(bf16[4,8,48,384]{3,2,1,0:T(8,128)(2,1)} %all-to-all-done.4.refs_1_), channel_id=1, source_target_pairs={{8,16},{10,18},{12,20},{14,22},{16,8},{18,10},{20,12},{22,14},{9,1... | collective-permute-start | bytes 3538952 | tf_op jit(solution)/shard_map/send_a1/ppermute | solution.py:364
  130.2 53.2 %collective-permute-start.14 = (bf16[4,8,48,384]{3,2,1,0:T(8,128)(2,1)}, bf16[4,8,48,384]{3,2,1,0:T(8,128)(2,1)}, u32[]{:S(2)}, u32[]{:S(2)}) collective-permute-start(bf16[4,8,48,384]{3,2,1,0:T(8,128)(2,1)} %all-to-all-done.5.refs_5_), channel_id=1, source_target_pairs={{0,8},{2,10},{4,12},{6,14},{24,16},{26,18},{28,20},{30,22},{1,9},{... | collective-permute-start | bytes 3538952 | tf_op jit(solution)/shard_map/send_v1/ppermute | solution.py:364
  137.5 50.9 %collective-permute-start = (bf16[4,8,48,384]{3,2,1,0:T(8,128)(2,1)}, bf16[4,8,48,384]{3,2,1,0:T(8,128)(2,1)}, u32[]{:S(2)}, u32[]{:S(2)}) collective-permute-start(bf16[4,8,48,384]{3,2,1,0:T(8,128)(2,1)} %all-to-all-done.refs_1_), channel_id=1, source_target_pairs={{0,8},{2,10},{4,12},{6,14},{24,16},{26,18},{28,20},{30,22},{1,9},{... | collective-permute-start | bytes 3538952 | tf_op jit(solution)/shard_map/send_n2/ppermute | solution.py:364
  139.8 53.9 %collective-permute-start.13 = (bf16[4,8,48,384]{3,2,1,0:T(8,128)(2,1)}, bf16[4,8,48,384]{3,2,1,0:T(8,128)(2,1)}, u32[]{:S(2)}, u32[]{:S(2)}) collective-permute-start(bf16[4,8,48,384]{3,2,1,0:T(8,128)(2,1)} %collective-permute-done.11.refs_2_), channel_id=1, source_target_pairs={{8,16},{10,18},{12,20},{14,22},{16,8},{18,10},{20,12},{22,14},{9,1... | collective-permute-start | bytes 3538952 | tf_op jit(solution)/shard_map/send_b1/ppermute | solution.py:364
  167.3 54.1 %collective-permute-start.4 = (bf16[12,192,384]{2,1,0:T(8,128)(2,1)S(1)}, bf16[12,192,384]{2,1,0:T(8,128)(2,1)}, u32[]{:S(2)}, u32[]{:S(2)}) collective-permute-start(bf16[12,192,384]{2,1,0:T(8,128)(2,1)S(1)} %copy-done.1), channel_id=1, source_target_pairs={{0,1},{1,0},{2,3},{3,2},{4,5},{5,4},{6,7},{7,6},{8,9},{9,8},{10,11... | collective-permute-start | bytes 5308424 | tf_op jit(solution)/shard_map/send_y2/ppermute | solution.py:364
  181.7 58.6 %collective-permute-start.1 = (bf16[4,8,48,384]{3,2,1,0:T(8,128)(2,1)}, bf16[4,8,48,384]{3,2,1,0:T(8,128)(2,1)}, u32[]{:S(2)}, u32[]{:S(2)}) collective-permute-start(bf16[4,8,48,384]{3,2,1,0:T(8,128)(2,1)} %all-to-all-done.refs_1_), channel_id=1, source_target_pairs={{8,16},{10,18},{12,20},{14,22},{16,8},{18,10},{20,12},{22,14},{9,1... | collective-permute-start | bytes 3538952 | tf_op jit(solution)/shard_map/send_a2/ppermute | solution.py:364
  183.4 56.9 %collective-permute-start.3 = (bf16[4,8,48,384]{3,2,1,0:T(8,128)(2,1)}, bf16[4,8,48,384]{3,2,1,0:T(8,128)(2,1)}, u32[]{:S(2)}, u32[]{:S(2)}) collective-permute-start(bf16[4,8,48,384]{3,2,1,0:T(8,128)(2,1)} %all-to-all-done.1.refs_5_), channel_id=1, source_target_pairs={{0,8},{2,10},{4,12},{6,14},{24,16},{26,18},{28,20},{30,22},{1,9},{... | collective-permute-start | bytes 3538952 | tf_op jit(solution)/shard_map/send_v2/ppermute | solution.py:364
  188.4 51.9 %collective-permute-start.2 = (bf16[4,8,48,384]{3,2,1,0:T(8,128)(2,1)}, bf16[4,8,48,384]{3,2,1,0:T(8,128)(2,1)}, u32[]{:S(2)}, u32[]{:S(2)}) collective-permute-start(bf16[4,8,48,384]{3,2,1,0:T(8,128)(2,1)} %collective-permute-done.refs_2_), channel_id=1, source_target_pairs={{8,16},{10,18},{12,20},{14,22},{16,8},{18,10},{20,12},{22,14},{9,1... | collective-permute-start | bytes 3538952 | tf_op jit(solution)/shard_map/send_b2/ppermute | solution.py:364
  220.8 69.2 %collective-permute-start.22 = (bf16[12,192,384]{2,1,0:T(8,128)(2,1)S(1)}, bf16[12,192,384]{2,1,0:T(8,128)(2,1)}, u32[]{:S(2)}, u32[]{:S(2)}) collective-permute-start(bf16[12,192,384]{2,1,0:T(8,128)(2,1)S(1)} %copy-done), channel_id=1, source_target_pairs={{0,1},{1,0},{2,3},{3,2},{4,5},{5,4},{6,7},{7,6},{8,9},{9,8},{10,11... | collective-permute-start | bytes 5308424 | tf_op jit(solution)/shard_map/send_y3/ppermute | solution.py:364
  288.4 39.9 %collective-permute-start.24 = (bf16[4,8,48,384]{3,2,1,0:T(8,128)(2,1)}, bf16[4,8,48,384]{3,2,1,0:T(8,128)(2,1)}, u32[]{:S(2)}, u32[]{:S(2)}) collective-permute-start(bf16[4,8,48,384]{3,2,1,0:T(8,128)(2,1)} %all-to-all-done.11.refs_1_), channel_id=1, source_target_pairs={{8,16},{10,18},{12,20},{14,22},{16,8},{18,10},{20,12},{22,14},{9,1... | collective-permute-start | bytes 3538952 | tf_op jit(solution)/shard_map/send_a3/ppermute | solution.py:364
  290.1 39.9 %collective-permute-start.26 = (bf16[4,8,48,384]{3,2,1,0:T(8,128)(2,1)}, bf16[4,8,48,384]{3,2,1,0:T(8,128)(2,1)}, u32[]{:S(2)}, u32[]{:S(2)}) collective-permute-start(bf16[4,8,48,384]{3,2,1,0:T(8,128)(2,1)} %copy-done.18), channel_id=1, source_target_pairs={{0,8},{2,10},{4,12},{6,14},{24,16},{26,18},{28,20},{30,22},{1,9},{... | collective-permute-start | bytes 3538952 | tf_op jit(solution)/shard_map/send_v3/ppermute | solution.py:364
  299.3 53.0 %collective-permute-start.27 = (bf16[4,8,48,384]{3,2,1,0:T(8,128)(2,1)}, bf16[4,8,48,384]{3,2,1,0:T(8,128)(2,1)}, u32[]{:S(2)}, u32[]{:S(2)}) collective-permute-start(bf16[4,8,48,384]{3,2,1,0:T(8,128)(2,1)} %all-to-all-done.13.refs_1_), channel_id=1, source_target_pairs={{0,8},{2,10},{4,12},{6,14},{24,16},{26,18},{28,20},{30,22},{1,9},{... | collective-permute-start | bytes 3538952 | tf_op jit(solution)/shard_map/send_n4/ppermute | solution.py:364
  301.8 59.5 %collective-permute-start.25 = (bf16[4,8,48,384]{3,2,1,0:T(8,128)(2,1)}, bf16[4,8,48,384]{3,2,1,0:T(8,128)(2,1)}, u32[]{:S(2)}, u32[]{:S(2)}) collective-permute-start(bf16[4,8,48,384]{3,2,1,0:T(8,128)(2,1)} %collective-permute-done.23.refs_2_), channel_id=1, source_target_pairs={{8,16},{10,18},{12,20},{14,22},{16,8},{18,10},{20,12},{22,14},{9,1... | collective-permute-start | bytes 3538952 | tf_op jit(solution)/shard_map/send_b3/ppermute | solution.py:364
  305.9 51.9 %all-to-all-start.10 = ((bf16[4,8,48,384]{3,2,1,0:T(8,128)(2,1)}), bf16[4,8,48,384]{3,2,1,0:T(8,128)(2,1)S(1)}, u32[]{:S(2)}, u32[]{:S(2)}) async-start(bf16[4,8,48,384]{3,2,1,0:T(8,128)(2,1)} %broadcast_select_fusion.3), calls=%async_computation.10 | async-start | bytes 2359296 | tf_op jit(solution)/shard_map/share_r0/all_to_all | solution.py:369
  324.4 56.1 %collective-permute-start.19 = (bf16[4,8,48,384]{3,2,1,0:T(8,128)(2,1)}, bf16[4,8,48,384]{3,2,1,0:T(8,128)(2,1)}, u32[]{:S(2)}, u32[]{:S(2)}) collective-permute-start(bf16[4,8,48,384]{3,2,1,0:T(8,128)(2,1)} %get-tuple-element.75), channel_id=1, source_target_pairs={{8,0},{10,2},{12,4},{14,6},{16,24},{18,26},{20,28},{22,30},{9,1},{... | collective-permute-start | bytes 3538952 | tf_op jit(solution)/shard_map/send_o2/ppermute | solution.py:364
  328.2 61.2 %collective-permute-start.28 = (bf16[4,8,48,384]{3,2,1,0:T(8,128)(2,1)}, bf16[4,8,48,384]{3,2,1,0:T(8,128)(2,1)}, u32[]{:S(2)}, u32[]{:S(2)}) collective-permute-start(bf16[4,8,48,384]{3,2,1,0:T(8,128)(2,1)} %all-to-all-done.13.refs_1_), channel_id=1, source_target_pairs={{8,16},{10,18},{12,20},{14,22},{16,8},{18,10},{20,12},{22,14},{9,1... | collective-permute-start | bytes 3538952 | tf_op jit(solution)/shard_map/send_a4/ppermute | solution.py:364
  329.9 61.2 %collective-permute-start.30 = (bf16[4,8,48,384]{3,2,1,0:T(8,128)(2,1)S(1)}, bf16[4,8,48,384]{3,2,1,0:T(8,128)(2,1)}, u32[]{:S(2)}, u32[]{:S(2)}) collective-permute-start(bf16[4,8,48,384]{3,2,1,0:T(8,128)(2,1)S(1)} %copy-done.17), channel_id=1, source_target_pairs={{0,8},{2,10},{4,12},{6,14},{24,16},{26,18},{28,20},{30,22},{1,9},{... | collective-permute-start | bytes 3538952 | tf_op jit(solution)/shard_map/send_v4/ppermute | solution.py:364
  352.3 50.6 %collective-permute-start.15 = (bf16[4,8,48,384]{3,2,1,0:T(8,128)(2,1)}, bf16[4,8,48,384]{3,2,1,0:T(8,128)(2,1)}, u32[]{:S(2)}, u32[]{:S(2)}) collective-permute-start(bf16[4,8,48,384]{3,2,1,0:T(8,128)(2,1)} %all-to-all-done.6.refs_1_), channel_id=1, source_target_pairs={{0,8},{2,10},{4,12},{6,14},{24,16},{26,18},{28,20},{30,22},{1,9},{... | collective-permute-start | bytes 3538952 | tf_op jit(solution)/shard_map/send_n5/ppermute | solution.py:364
  357.7 39.4 %all-to-all-start.9 = ((bf16[4,8,48,384]{3,2,1,0:T(8,128)(2,1)}), bf16[4,8,48,384]{3,2,1,0:T(8,128)(2,1)S(1)}, u32[]{:S(2)}, u32[]{:S(2)}) async-start(bf16[4,8,48,384]{3,2,1,0:T(8,128)(2,1)} %broadcast_select_fusion.4), calls=%async_computation.9 | async-start | bytes 2359296 | tf_op jit(solution)/shard_map/share_r1/all_to_all | solution.py:369
  361.3 43.3 %collective-permute-start.29 = (bf16[4,8,48,384]{3,2,1,0:T(8,128)(2,1)}, bf16[4,8,48,384]{3,2,1,0:T(8,128)(2,1)}, u32[]{:S(2)}, u32[]{:S(2)}) collective-permute-start(bf16[4,8,48,384]{3,2,1,0:T(8,128)(2,1)} %collective-permute-done.27.refs_2_), channel_id=1, source_target_pairs={{8,16},{10,18},{12,20},{14,22},{16,8},{18,10},{20,12},{22,14},{9,1... | collective-permute-start | bytes 3538952 | tf_op jit(solution)/shard_map/send_b4/ppermute | solution.py:364
  380.5 54.3 %collective-permute-start.33 = (bf16[4,8,48,384]{3,2,1,0:T(8,128)(2,1)}, bf16[4,8,48,384]{3,2,1,0:T(8,128)(2,1)}, u32[]{:S(2)}, u32[]{:S(2)}) collective-permute-start(bf16[4,8,48,384]{3,2,1,0:T(8,128)(2,1)} %get-tuple-element.97), channel_id=1, source_target_pairs={{8,0},{10,2},{12,4},{14,6},{16,24},{18,26},{20,28},{22,30},{9,1},{... | collective-permute-start | bytes 3538952 | tf_op jit(solution)/shard_map/send_o3/ppermute | solution.py:364
  389.4 51.5 %collective-permute-start.16 = (bf16[4,8,48,384]{3,2,1,0:T(8,128)(2,1)}, bf16[4,8,48,384]{3,2,1,0:T(8,128)(2,1)}, u32[]{:S(2)}, u32[]{:S(2)}) collective-permute-start(bf16[4,8,48,384]{3,2,1,0:T(8,128)(2,1)} %all-to-all-done.6.refs_1_), channel_id=1, source_target_pairs={{8,16},{10,18},{12,20},{14,22},{16,8},{18,10},{20,12},{22,14},{9,1... | collective-permute-start | bytes 3538952 | tf_op jit(solution)/shard_map/send_a5/ppermute | solution.py:364
  391.2 49.8 %collective-permute-start.18 = (bf16[4,8,48,384]{3,2,1,0:T(8,128)(2,1)}, bf16[4,8,48,384]{3,2,1,0:T(8,128)(2,1)}, u32[]{:S(2)}, u32[]{:S(2)}) collective-permute-start(bf16[4,8,48,384]{3,2,1,0:T(8,128)(2,1)} %all-to-all-done.7.refs_5_), channel_id=1, source_target_pairs={{0,8},{2,10},{4,12},{6,14},{24,16},{26,18},{28,20},{30,22},{1,9},{... | collective-permute-start | bytes 3538952 | tf_op jit(solution)/shard_map/send_v5/ppermute | solution.py:364
  402.9 38.1 %collective-permute-start.17 = (bf16[4,8,48,384]{3,2,1,0:T(8,128)(2,1)}, bf16[4,8,48,384]{3,2,1,0:T(8,128)(2,1)}, u32[]{:S(2)}, u32[]{:S(2)}) collective-permute-start(bf16[4,8,48,384]{3,2,1,0:T(8,128)(2,1)} %collective-permute-done.15.refs_2_), channel_id=1, source_target_pairs={{8,16},{10,18},{12,20},{14,22},{16,8},{18,10},{20,12},{22,14},{9,1... | collective-permute-start | bytes 3538952 | tf_op jit(solution)/shard_map/send_b5/ppermute | solution.py:364
  421.7 37.8 %collective-permute-start.32 = (bf16[4,8,48,384]{3,2,1,0:T(8,128)(2,1)}, bf16[4,8,48,384]{3,2,1,0:T(8,128)(2,1)S(1)}, u32[]{:S(2)}, u32[]{:S(2)}) collective-permute-start(bf16[4,8,48,384]{3,2,1,0:T(8,128)(2,1)} %get-tuple-element.96), channel_id=1, source_target_pairs={{8,0},{10,2},{12,4},{14,6},{16,24},{18,26},{20,28},{22,30},{9,1},{... | collective-permute-start | bytes 3538952 | tf_op jit(solution)/shard_map/send_o4/ppermute | solution.py:364
  (39 other events, 724.7 us)
